TPU v7x, 128 devices: a whole 4x4x4 slice. The times are simulated.
128 devices in a mesh: dp: 16 (over x, z), group: 8 (over y, core).
Axes of the slice: x: 4, y: 4, z: 4, core: 2. Of those that a mesh axis runs over, the one named last changes fastest.
Arguments:
- acts: bfloat16 [8192, 4096], P('dp', 'group'), may hold values from -9 to 9
- grads_out: bfloat16 [8192, 16384], P('dp', 'group'), may hold values from -1 to 1
- owners: int32 [16, 16, 1], P('dp'), may hold values from 0 to 7; in each aligned block of 16 rows (0 to 15, 16 to 31, ..., all dimensions but the last counted through in order) at most 3 rows name the same one
- left_stats: float32 [16, 8, 3, 512, 512], P('dp', 'group'), may hold values from -1 to 4
- right_stats: float32 [16, 8, 3, 512, 512], P('dp', 'group'), may hold values from -1 to 4
- left_root: bfloat16 [16, 8, 3, 512, 512], P('dp', 'group'), may hold values from -1 to 3
- right_root: bfloat16 [16, 8, 3, 512, 512], P('dp', 'group'), may hold values from -1 to 3
Outputs:
- left_new: float32 [16, 8, 3, 512, 512], P('dp', 'group')
- right_new: float32 [16, 8, 3, 512, 512], P('dp', 'group')
- update: bfloat16 [256, 512, 512], P(('group', 'dp'))
Inputs may be any that keep to these rules, and one draw needn't show every extreme that they name: `owners`: in the 16 rows of one dp index no owner is named more than 3 times.
All inputs are finite; a program needn't handle non-finite values.
Results may differ from a plain program's by a relative error of at most 0.029.
Values may be sent and summed in bfloat16 or wider, within the bound.
A program may use at most 192 MiB of HBM per device.

v0:
```python
import jax
import jax.numpy as jnp
from jax import lax
from jax.sharding import PartitionSpec as P

STAT_DECAY = 0.9
EPSILON = 1e-06


def precondition(left_fourth, blocks, right_fourth):
    shaped = jnp.einsum(
        "sab,sbc->sac", left_fourth, blocks, preferred_element_type=jnp.float32
    ).astype(jnp.bfloat16)
    product = jnp.einsum("sab,sbc->sac", shaped, right_fourth, preferred_element_type=jnp.float32)
    scaling = lax.rsqrt(jnp.mean(product * product, axis=(1, 2), keepdims=True) + EPSILON)
    return (product * scaling).astype(jnp.bfloat16)


def body(acts, grads_out, owners, left_stats, right_stats, left_root, right_root):
    block_size = left_stats.shape[-1]
    capacity = left_stats.shape[2]
    tok_rows = acts.shape[0]
    gathered = lax.all_gather(acts, "group", axis=1, tiled=True)
    col_blocks = gathered.shape[1] // block_size
    slab_rows = grads_out.shape[1] // block_size
    per_device = slab_rows * col_blocks // lax.axis_size("dp")
    out_blocks = grads_out.reshape(tok_rows, slab_rows, block_size)
    in_blocks = gathered.reshape(tok_rows, col_blocks, block_size)
    block_ids = jnp.arange(per_device * lax.axis_size("dp"), dtype=jnp.int32)
    left_part = jnp.take(out_blocks, block_ids // col_blocks, axis=1)
    right_part = jnp.take(in_blocks, block_ids % col_blocks, axis=1)
    summed = lax.psum_scatter(
        jnp.einsum(
            "tcf,tcd->cfd", left_part, right_part, preferred_element_type=jnp.float32
        ).astype(jnp.bfloat16),
        "dp",
        scatter_dimension=0,
        tiled=True,
    )
    my_index = lax.axis_index("group")
    owner_list = owners[0, :, 0]
    row_count = owner_list.shape[0]
    position = jnp.arange(row_count, dtype=jnp.int32)
    matches = owner_list[:, None] == owner_list[None, :]
    earlier = position[None, :] < position[:, None]
    slot_of = jnp.sum((matches & earlier).astype(jnp.int32), axis=1)
    slot_range = jnp.arange(capacity, dtype=jnp.int32)

    def selector(block_ids):
        mine_flag = jnp.take(owner_list, block_ids) == my_index
        fitting = jnp.take(slot_of, block_ids)[:, None] == slot_range[None, :]
        return (mine_flag[:, None] & fitting).astype(jnp.bfloat16)

    piece = lax.all_gather(summed, "group", axis=0, tiled=True)
    block_ids = jnp.arange(piece.shape[0], dtype=jnp.int32)
    picked = jnp.einsum(
        "ks,kab->sab", selector(block_ids), piece, preferred_element_type=jnp.float32
    )
    owned = picked.astype(jnp.bfloat16)
    left_gram = jnp.einsum("sab,scb->sac", owned, owned, preferred_element_type=jnp.float32)
    right_gram = jnp.einsum("sab,sac->sbc", owned, owned, preferred_element_type=jnp.float32)
    left_new = STAT_DECAY * left_stats + (1.0 - STAT_DECAY) * left_gram[None, None]
    right_new = STAT_DECAY * right_stats + (1.0 - STAT_DECAY) * right_gram[None, None]
    slot_results = precondition(left_root[0, 0], owned, right_root[0, 0])
    block_ids = jnp.arange(per_device * lax.axis_size("group"), dtype=jnp.int32)
    update = lax.psum_scatter(
        jnp.einsum(
            "ks,sab->kab", selector(block_ids), slot_results, preferred_element_type=jnp.float32
        ).astype(jnp.bfloat16),
        "group",
        scatter_dimension=0,
        tiled=True,
    )
    return (left_new, right_new, update)


def solution(mesh):
    placed = (
        P("dp", "group"),
        P("dp", "group"),
        P("dp", None, None),
        P("dp", "group", None, None, None),
        P("dp", "group", None, None, None),
        P("dp", "group", None, None, None),
        P("dp", "group", None, None, None),
    )
    return jax.shard_map(
        body,
        mesh=mesh,
        in_specs=placed,
        out_specs=(
            P("dp", "group", None, None, None),
            P("dp", "group", None, None, None),
            P(("group", "dp"), None, None),
        ),
        check_vma=False,
    )
```

profile of v0, /device:TPU:1, one launch (start us, length us, event | category | flops | bytes accessed | tf_op | source)
XLA Modules:
  0.0 338.6 jit_solution(12147439124417944006)
XLA Ops:
  7.2 2.2 copy.66
  9.4 0.0 reduce-scatter.3.cloned.1.call-start
  9.5 3.9 %copy.64 = bf16[512,2048]{0,1:T(8,128)(2,1)} copy(bf16[512,2048]{1,0:T(8,128)(2,1)} %param.10) | data formatting | bytes 4194304 | tf_op args[1]
  13.4 4.1 %copy.65 = bf16[512,4,512]{2,0,1:T(8,128)(2,1)} copy(bf16[512,4,512]{0,2,1:T(8,128)(2,1)} %bitcast.39) | data formatting | bytes 4194304 | tf_op jit(solution)/shard_map/reshape | solution.py:27
  17.5 9.0 %gather_fusion = bf16[32,512,512]{2,1,0:T(8,128)(2,1)} fusion(bf16[512,4,512]{2,0,1:T(8,128)(2,1)} %copy.65, s32[1024]{0:T(1024)S(1)} %pad_clamp_fusion.1), kind=kCustom, calls=%fused_computation.2 | custom fusion | bytes 33554560 | tf_op jit(solution)/shard_map/jit(_take)/gather | solution.py:30
  26.6 19.5 %all-gather.3.cloned.1.call-done = bf16[512,4096]{0,1:T(8,128)(2,1)} async-done(((bf16[512,512]{0,1:T(8,128)(2,1)}), bf16[512,4096]{0,1:T(8,128)(2,1)}) %all-gather.3.cloned.1.call-update) | async-done | bytes 4194320 | tf_op jit(solution)/shard_map/all_gather | solution.py:23
  46.1 6.4 %copy.67 = bf16[512,8,512]{2,0,1:T(8,128)(2,1)} copy(bf16[512,8,512]{0,2,1:T(8,128)(2,1)} %bitcast.40) | data formatting | bytes 8388608 | tf_op jit(solution)/shard_map/reshape | solution.py:28
  52.5 9.2 %gather_fusion.1 = bf16[32,512,512]{2,1,0:T(8,128)(2,1)} fusion(bf16[512,8,512]{2,0,1:T(8,128)(2,1)} %copy.67, s32[1024]{0:T(1024)S(1)} %pad_clamp_fusion), kind=kCustom, calls=%fused_computation.3 | custom fusion | bytes 33554560 | tf_op jit(solution)/shard_map/jit(_take)/gather | solution.py:31
  61.7 22.0 %fusion.7 = bf16[32,512,512]{2,1,0:T(8,128)(2,1)} fusion(bf16[32,512,512]{2,1,0:T(8,128)(2,1)} %gather_fusion.1, pred[32]{0:T(512)(128)(4,1)S(1)} %get-tuple-element.15, bf16[32,512,512]{2,1,0:T(8,128)(2,1)} %gather_fusion, pred[32]{0:T(512)(128)(4,1)S(1)} %get-tuple-element.16), kind=kOutput, calls=%fused_computation.11 | convolution fusion | flops 8615100416 | bytes 50331712 | tf_op jit(solution)/shard_map/tcf,tcd->cfd/dot_general | solution.py:33
  83.7 0.0 all-gather.5.cloned.1.call-start
  83.8 110.0 %reduce-scatter.3.cloned.1.call-done = bf16[2,512,512]{2,1,0:T(8,128)(2,1)} async-done(((bf16[32,512,512]{2,1,0:T(8,128)(2,1)}), bf16[2,512,512]{2,1,0:T(8,128)(2,1)}) %reduce-scatter.3.cloned.1.call-update) | async-done | bytes 1048592 | tf_op jit(solution)/shard_map/reduce_scatter | solution.py:32
  193.8 0.2 reduce-scatter.5.cloned.1.call-start
  194.1 0.7 gather_fusion.2
  194.7 0.2 convert_reduce_fusion
  194.9 0.7 gather_fusion.3
  195.6 49.8 %all-gather.5.cloned.1.call-done = bf16[16,512,512]{2,1,0:T(8,128)(2,1)} async-done(((bf16[2,512,512]{2,1,0:T(8,128)(2,1)}), bf16[16,512,512]{2,1,0:T(8,128)(2,1)}) %all-gather.5.cloned.1.call-update) | async-done | bytes 8388624 | tf_op jit(solution)/shard_map/all_gather | solution.py:54
  245.4 9.8 %fusion.12 = bf16[3,512,512]{2,0,1:T(4,128)(2,1)} fusion(bf16[16,512,512]{2,1,0:T(8,128)(2,1)} %all-gather.5.cloned.1.call-done, s32[16]{0:T(128)S(1)} %compare_select_fusion.4, pred[16]{0:T(512)(128)(4,1)S(1)} %fusion.26), kind=kOutput, calls=%fused_computation.12 | convolution fusion | flops 25165920 | bytes 9961552 | tf_op jit(solution)/shard_map/ks,kab->sab/dot_general | solution.py:56
  255.2 5.5 %multiply_reduce_fusion = (f32[3]{0:T(128)S(1)}, f32[3,512,512]{2,1,0:T(8,128)}) fusion(bf16[1,1,3,512,512]{4,3,2,1,0:T(8,128)(2,1)S(1)} %copy-done, bf16[1,1,3,512,512]{4,3,2,1,0:T(8,128)(2,1)S(1)} %copy-done.4, bf16[3,512,512]{2,0,1:T(4,128)(2,1)} %fusion.12), kind=kOutput, calls=%fused_computation.20 | convolution fusion | flops 1612972032 | bytes 7864332 | tf_op jit(solution)/shard_map/sab,sbc->sac/dot_general | solution.py:14
  260.7 2.4 multiply_convert_fusion
  263.0 5.8 %convolution_convert_fusion = bf16[16,512,512]{2,0,1:T(8,128)(2,1)} fusion(bf16[3,512,512]{2,1,0:T(8,128)(2,1)S(1)} %multiply_convert_fusion, s32[16]{0:T(128)S(1)} %compare_select_fusion.4, pred[16]{0:T(512)(128)(4,1)S(1)} %fusion.26), kind=kOutput, calls=%fused_computation.15 | convolution fusion | flops 29360224 | bytes 9961552 | tf_op jit(solution)/shard_map/ks,sab->kab/dot_general | solution.py:67
  268.9 11.4 %copy.75 = bf16[16,512,512]{2,1,0:T(8,128)(2,1)} copy(bf16[16,512,512]{2,0,1:T(8,128)(2,1)} %convolution_convert_fusion) | data formatting | bytes 16777216 | tf_op jit(solution)/shard_map/convert_element_type | solution.py:69
  280.3 6.3 %bitcast_add_fusion.1 = f32[1,1,3,512,512]{4,3,2,1,0:T(8,128)} fusion(f32[1,1,3,512,512]{4,3,2,1,0:T(8,128)} %param.12, bf16[3,512,512]{2,0,1:T(4,128)(2,1)} %fusion.12), kind=kOutput, calls=%fused_computation.17 | convolution fusion | flops 807665664 | bytes 7864320 | tf_op jit(solution)/shard_map/sab,scb->sac/dot_general | solution.py:60
  286.6 3.2 bitcast_add_fusion
  289.9 42.2 %reduce-scatter.5.cloned.1.call-done = bf16[2,512,512]{2,1,0:T(8,128)(2,1)} async-done(((bf16[16,512,512]{2,1,0:T(8,128)(2,1)}), bf16[2,512,512]{2,1,0:T(8,128)(2,1)}) %reduce-scatter.5.cloned.1.call-update) | async-done | bytes 1048592 | tf_op jit(solution)/shard_map/reduce_scatter | solution.py:66
  (25 shorter events, 0.2 us)
Async XLA Ops:
  7.2 248.0 %copy-start = (bf16[1,1,3,512,512]{4,3,2,1,0:T(8,128)(2,1)S(1)}, bf16[1,1,3,512,512]{4,3,2,1,0:T(8,128)(2,1)}, u32[]{:S(2)}) copy-start(bf16[1,1,3,512,512]{4,3,2,1,0:T(8,128)(2,1)} %param.15) | copy-start | bytes 4718596
  7.2 38.9 %all-gather.3.cloned.1.call-start = ((), (), s32[]{:S(2)}) async-start(), calls=%async_computation.2 | async-start | bytes 4718592 | tf_op jit(solution)/shard_map/all_gather | solution.py:23
  9.4 184.4 %reduce-scatter.3.cloned.1.call-start = ((), (), s32[]{:S(2)}) async-start(), calls=%async_computation.3 | async-start | bytes 17825792 | tf_op jit(solution)/shard_map/reduce_scatter | solution.py:32
  83.7 110.3 %copy-start.1 = (s32[1,16,1]{1,2,0:T(1,128)S(1)}, s32[1,16,1]{1,2,0:T(1,128)}, u32[]{:S(2)}) copy-start(s32[1,16,1]{1,2,0:T(1,128)} %param.11) | copy-start | bytes 196
  83.7 161.7 %all-gather.5.cloned.1.call-start = ((), (), s32[]{:S(2)}) async-start(), calls=%async_computation.4 | async-start | bytes 9437184 | tf_op jit(solution)/shard_map/all_gather | solution.py:54
  193.8 138.3 %reduce-scatter.5.cloned.1.call-start = ((), (), s32[]{:S(2)}) async-start(), calls=%async_computation.5 | async-start | bytes 9437184 | tf_op jit(solution)/shard_map/reduce_scatter | solution.py:66
  195.6 59.6 %copy-start.4 = (bf16[1,1,3,512,512]{4,3,2,1,0:T(8,128)(2,1)S(1)}, bf16[1,1,3,512,512]{4,3,2,1,0:T(8,128)(2,1)}, u32[]{:S(2)}) copy-start(bf16[1,1,3,512,512]{4,3,2,1,0:T(8,128)(2,1)} %param.14) | copy-start | bytes 4718596
  280.3 6.4 %copy-start.2 = (bf16[3,512,512]{2,0,1:T(4,128)(2,1)S(1)}, bf16[3,512,512]{2,0,1:T(4,128)(2,1)}, u32[]{:S(2)}) copy-start(bf16[3,512,512]{2,0,1:T(4,128)(2,1)} %fusion.12) | copy-start | bytes 4718596
  280.3 6.3 %copy-start.3 = (f32[1,1,3,512,512]{4,3,2,1,0:T(8,128)S(1)}, f32[1,1,3,512,512]{4,3,2,1,0:T(8,128)}, u32[]{:S(2)}) copy-start(f32[1,1,3,512,512]{4,3,2,1,0:T(8,128)} %param.13) | copy-start | bytes 9437188
Sparse Core Ops, SparseCore 0:
  10.3 35.7 all-gather.2
  83.8 109.8 reduce-scatter.2
  195.5 49.8 all-gather.4
  280.4 51.5 reduce-scatter.4
where the time goes:
time: 339 us
  waiting for transfers between devices  222 us (65%)
  matrix products  52.6 us (16%)
  local copies, waits for them, and re-layouts  47.6 us (14%)
  between operations  13.9 us (4%)
    reduce_scatter x1, waiting for transfers between devices, body(): lax.psum_scatter(jnp.einsum('tcf,tcd->cfd', left_part, right_part, prefer...  110 us
    all_gather x1, waiting for transfers between devices, body(): piece = lax.all_gather(summed, 'group', axis=0, tiled=True)  49.8 us
    reduce_scatter x1, waiting for transfers between devices, body(): lax.psum_scatter(jnp.einsum('ks,sab->kab', selector(block_ids), slot_resu...  42.2 us
    dot_general x1, matrix products, body(): jnp.einsum('tcf,tcd->cfd', left_part, right_part, preferred_element_type=...  22 us
    all_gather x1, waiting for transfers between devices, body(): gathered = lax.all_gather(acts, 'group', axis=1, tiled=True)  19.5 us
    convert_element_type x1, local copies, waits for them, and re-layouts, body(): update = lax.psum_scatter(jnp.einsum('ks,sab->kab', selector(block_ids),...  11.4 us
    dot_general x1, matrix products, body(): jnp.einsum('ks,kab->sab', selector(block_ids), piece, preferred_element_t...  9.77 us
    gather x1, local copies, waits for them, and re-layouts, body(): right_part = jnp.take(in_blocks, block_ids % col_blocks, axis=1)  9.17 us
  transfers between devices with their start and end apart: 4, of which 4 were waited for; matrix products, arithmetic and copies ran while one was open for 8% of the time, Pallas kernels for 0%

commit v1 on v0

v1 whole, which is shorter than its diff:
```python
import functools

import jax
import jax.numpy as jnp
from jax import lax
from jax.experimental import pallas as pl
from jax.experimental.pallas import tpu as pltpu
from jax.sharding import PartitionSpec as P

MESH = pl.DeviceIdType.MESH
STAT_DECAY = 0.9
EPSILON = 1e-06
BLK = 512
SIDE = 4
ROUNDS = 4
PART = BLK // 4
F32 = jnp.float32
BF16 = jnp.bfloat16


def place():
    dp, group = lax.axis_index("dp"), lax.axis_index("group")
    return dp // SIDE, group // 2, lax.rem(dp, SIDE), lax.rem(group, 2)


def ring(index, step):
    return lax.rem(index + step + SIDE, SIDE)


def device(x, y, z, core):
    return (x * SIDE + z, y * 2 + core)


def remote(src, dst, send, recv, target):
    return pltpu.make_async_remote_copy(
        src_ref=src, dst_ref=dst, send_sem=send, recv_sem=recv, device_id=target, device_id_type=MESH
    )


def greet(targets):
    barrier = pltpu.get_barrier_semaphore()
    for target in targets:
        pl.semaphore_signal(barrier, inc=1, device_id=target, device_id_type=MESH)
    pl.semaphore_wait(barrier, len(targets))


def plus(*terms):
    total = terms[0].astype(F32)
    for term in terms[1:]:
        total = total + term.astype(F32)
    return total.astype(BF16)


class RingSum:
    def __init__(self, part, me, right, left, far, near, send, recv):
        self.part, self.me = part, me
        to_right = [
            (part(ring(me, 2)).at[0], far.at[0]),
            (part(ring(me, 1)).at[1], near.at[0, 1]),
            (part(ring(me, 1)).at[0], near.at[0, 0]),
        ]
        to_left = [
            (part(ring(me, 2)).at[1], far.at[1]),
            (part(ring(me, -1)).at[0], near.at[1, 0]),
            (part(ring(me, -1)).at[1], near.at[1, 1]),
        ]
        self.far, self.near = far, near
        self.copies = []
        for i in range(3):
            for j, (target, lists) in enumerate(((right, to_right), (left, to_left))):
                src, dst = lists[i]
                self.copies.append(remote(src, dst, send.at[2 * i + j], recv.at[2 * i + j], target))

    def first(self):
        for copy in self.copies[:4]:
            copy.start()

    def merge(self):
        for j, (step, half) in enumerate(((1, 0), (-1, 1))):
            self.copies[j].wait_recv()
            ref = self.part(ring(self.me, step)).at[half]
            ref[...] = plus(ref[...], self.far[j])
            self.copies[4 + j].start()

    def total(self):
        for copy in self.copies[2:]:
            copy.wait_recv()
        mine = self.part(self.me)
        return [plus(mine[half], self.near[0, half], self.near[1, half]) for half in range(2)]

    def finish(self):
        for copy in self.copies:
            copy.wait_send()


def reduce_kernel(
    acts_ref, grads_ref, all_ref,
    grads, turned, acts, parts, far1, near1, sums, far2, near2, done,
    local_sem, acts_send, acts_recv, pair_send, pair_recv,
    send1, recv1, send2, recv2, out_send, out_recv, cross_send, cross_recv,
):
    x, y, z, core = place()
    other = 1 - core
    group = y * 2 + core
    partner = device(x, y, z, other)
    along_y = [device(x, ring(y, s), z, core) for s in (1, -1, 2)]
    along_x = [device(ring(x, s), y, z, core) for s in (1, -1)]
    along_z = [device(x, y, ring(z, s), core) for s in (1, -1)]

    load_grads = pltpu.make_async_copy(grads_ref, grads, local_sem.at[0])
    load_acts = pltpu.make_async_copy(acts_ref, acts.at[core, y], local_sem.at[1])
    load_grads.start()
    load_acts.start()
    greet([partner] + along_y + along_x + along_z)

    load_acts.wait()
    own = acts.at[core, y]
    acts_out = [remote(own, own, acts_send.at[i], acts_recv.at[i], along_y[i]) for i in range(3)]
    for copy in acts_out:
        copy.start()
    acts_pair = [remote(own, own, pair_send.at[0], pair_recv.at[0], partner)]
    acts_pair[0].start()
    load_grads.wait()
    for part in range(ROUNDS):
        for xd in range(SIDE):
            start = xd * BLK + part * PART
            turned[part, xd * PART : (xd + 1) * PART, :] = grads[:, start : start + PART].T
    for i, s in enumerate((-1, 1, 2)):
        acts_out[i].wait_recv()
        here = acts.at[core, ring(y, s)]
        copy = remote(here, here, pair_send.at[i + 1], pair_recv.at[i + 1], partner)
        copy.start()
        acts_pair.append(copy)

    def halves(ref):
        return ref

    stages1, stages2, outs, crosses = {}, {}, {}, {}

    def which(r):
        return lax.rem(core + r // 2, 2), r % 2

    def products(r):
        h, v = which(r)
        if r == 2:
            for copy in acts_pair:
                copy.wait_recv()
        for u in range(2):
            left = turned[v * 2 + u]

            def step(zd, carry, u=u, left=left):
                value = jnp.dot(left, acts[h, zd], preferred_element_type=F32).astype(BF16)
                for xd in range(SIDE):
                    piece = value[xd * PART : (xd + 1) * PART]
                    if u == 0:
                        parts[r, 0, xd, zd // 2, lax.rem(zd, 2)] = piece
                    else:
                        parts[r, 1, zd, xd // 2, xd % 2] = piece
                return carry

            lax.fori_loop(0, SIDE, step, 0)
            me, (right, left_to) = ((x, along_x), (z, along_z))[u]
            stage = RingSum(
                lambda d, u=u: parts.at[r, u, d], me, right, left_to,
                far1.at[r, u], near1.at[r, u], send1.at[r, u], recv1.at[r, u],
            )
            stage.first()
            stages1[r, u] = stage

    def merge1(r):
        for u in range(2):
            stages1[r, u].merge()

    def between(r):
        for u in range(2):
            total = stages1[r, u].total()
            for half in range(2):
                for o in range(2):
                    for piece in range(2):
                        sums[r, u, half * 2 + o, piece] = total[half][o, piece * (PART // 2) : (piece + 1) * (PART // 2)]
            me, (right, left_to) = ((z, along_z), (x, along_x))[u]
            stage = RingSum(
                lambda d, u=u: sums.at[r, u, d], me, right, left_to,
                far2.at[r, u], near2.at[r, u], send2.at[r, u], recv2.at[r, u],
            )
            stage.first()
            stages2[r, u] = stage

    def merge2(r):
        for u in range(2):
            stages2[r, u].merge()

    def spread(r):
        h, v = which(r)
        for u in range(2):
            total = stages2[r, u].total()
            for half in range(2):
                start = u * PART + half * (PART // 2)
                done[r, start : start + PART // 2] = total[half]
        rows = pl.ds(v * 2 * PART, 2 * PART)
        there = all_ref.at[2 * group + h, rows]
        keep = pltpu.make_async_copy(done.at[r], there, local_sem.at[2 + r])
        keep.start()
        outs[r] = [remote(done.at[r], there, out_send.at[r, i], out_recv.at[r, i], along_y[i]) for i in range(3)]
        for copy in outs[r]:
            copy.start()
        cross = remote(done.at[r], there, cross_send.at[r, 0], cross_recv.at[r, 0], partner)
        cross.start()
        crosses[r] = [cross]
        outs[r, "keep"] = keep

    def pass_on(r):
        h, v = which(r)
        rows = pl.ds(v * 2 * PART, 2 * PART)
        for i, s in enumerate((-1, 1, 2)):
            outs[r][i].wait_recv()
            here = all_ref.at[2 * (2 * ring(y, s) + core) + h, rows]
            cross = remote(here, here, cross_send.at[r, i + 1], cross_recv.at[r, i + 1], partner)
            cross.start()
            crosses[r].append(cross)

    for step in range(ROUNDS + 4):
        if step < ROUNDS:
            products(step)
        if 0 <= step - 2 < ROUNDS:
            spread(step - 2)
        if 0 <= step - 1 < ROUNDS:
            between(step - 1)
        if 0 <= step < ROUNDS:
            merge1(step)
        if 0 <= step - 1 < ROUNDS:
            merge2(step - 1)
        if 0 <= step - 3 < ROUNDS:
            pass_on(step - 3)

    for copy in acts_out + acts_pair:
        copy.wait_send()
    for r in range(ROUNDS):
        for u in range(2):
            stages1[r, u].finish()
            stages2[r, u].finish()
        for copy in outs[r]:
            copy.wait_send()
        outs[r, "keep"].wait()
        for copy in crosses[r]:
            copy.wait()


def reduce_blocks(acts, grads):
    dma = pltpu.SemaphoreType.DMA
    return pl.pallas_call(
        reduce_kernel,
        out_shape=jax.ShapeDtypeStruct((16, BLK, BLK), BF16),
        in_specs=[pl.BlockSpec(memory_space=pl.ANY)] * 2,
        out_specs=pl.BlockSpec(memory_space=pl.ANY),
        scratch_shapes=[
            pltpu.VMEM((BLK, 4 * BLK), BF16),
            pltpu.VMEM((ROUNDS, BLK, BLK), BF16),
            pltpu.VMEM((2, SIDE, BLK, BLK), BF16),
            pltpu.VMEM((ROUNDS, 2, SIDE, 2, 2, PART, BLK), BF16),
            pltpu.VMEM((ROUNDS, 2, 2, 2, PART, BLK), BF16),
            pltpu.VMEM((ROUNDS, 2, 2, 2, 2, PART, BLK), BF16),
            pltpu.VMEM((ROUNDS, 2, SIDE, 2, PART // 2, BLK), BF16),
            pltpu.VMEM((ROUNDS, 2, 2, PART // 2, BLK), BF16),
            pltpu.VMEM((ROUNDS, 2, 2, 2, PART // 2, BLK), BF16),
            pltpu.VMEM((ROUNDS, 2 * PART, BLK), BF16),
            dma((2 + ROUNDS,)),
            dma((3,)), dma((3,)), dma((4,)), dma((4,)),
            dma((ROUNDS, 2, 6)), dma((ROUNDS, 2, 6)),
            dma((ROUNDS, 2, 6)), dma((ROUNDS, 2, 6)),
            dma((ROUNDS, 3)), dma((ROUNDS, 3)),
            dma((ROUNDS, 4)), dma((ROUNDS, 4)),
        ],
        compiler_params=pltpu.CompilerParams(
            collective_id=0, has_side_effects=True, vmem_limit_bytes=60 << 20
        ),
        cost_estimate=pl.CostEstimate(flops=2 * 512 * 2048 * 4096, bytes_accessed=12 << 20, transcendentals=0),
        name="reduce_blocks",
    )(acts, grads)


def slot_kernel(index_ref, used_ref, block_ref, ls_ref, rs_ref, lr_ref, rr_ref, ln_ref, rn_ref, out_ref):
    used = used_ref[pl.program_id(0)]
    owned = jnp.where(used > 0, block_ref[0], jnp.zeros_like(block_ref[0]))
    shaped = jnp.dot(lr_ref[0, 0, 0], owned, preferred_element_type=F32).astype(BF16)
    product = jnp.dot(shaped, rr_ref[0, 0, 0], preferred_element_type=F32)
    scaling = lax.rsqrt(jnp.mean(product * product) + EPSILON)
    out_ref[0] = (product * scaling).astype(BF16)
    left = lax.dot_general(owned, owned, (((1,), (1,)), ((), ())), preferred_element_type=F32)
    ln_ref[0, 0, 0] = STAT_DECAY * ls_ref[0, 0, 0] + (1.0 - STAT_DECAY) * left
    right = lax.dot_general(owned, owned, (((0,), (0,)), ((), ())), preferred_element_type=F32)
    rn_ref[0, 0, 0] = STAT_DECAY * rs_ref[0, 0, 0] + (1.0 - STAT_DECAY) * right


def slots_step(index, used, blocks, left_stats, right_stats, left_root, right_root):
    capacity = left_stats.shape[2]
    whole = pl.BlockSpec((1, 1, 1, BLK, BLK), lambda s, index, used: (0, 0, s, 0, 0))
    return pl.pallas_call(
        slot_kernel,
        grid_spec=pltpu.PrefetchScalarGridSpec(
            num_scalar_prefetch=2,
            grid=(capacity,),
            in_specs=[pl.BlockSpec((1, BLK, BLK), lambda s, index, used: (index[s], 0, 0))] + [whole] * 4,
            out_specs=[whole, whole, pl.BlockSpec((1, BLK, BLK), lambda s, index, used: (s, 0, 0))],
        ),
        out_shape=[
            jax.ShapeDtypeStruct(left_stats.shape, F32),
            jax.ShapeDtypeStruct(right_stats.shape, F32),
            jax.ShapeDtypeStruct((capacity, BLK, BLK), BF16),
        ],
        compiler_params=pltpu.CompilerParams(vmem_limit_bytes=40 << 20),
        name="slots_step",
    )(index, used, blocks, left_stats, right_stats, left_root, right_root)


def return_kernel(owner_ref, slot_ref, slots_ref, out_ref, held, packed, far, near, pair_send, pair_recv, send, recv):
    x, y, z, core = place()
    partner = device(x, y, z, 1 - core)
    right, left = [device(x, ring(y, s), z, core) for s in (1, -1)]
    greet([partner, right, left])
    swap = remote(slots_ref, held, pair_send.at[0], pair_recv.at[0], partner)
    swap.start()

    def block(step, h):
        k = 2 * (2 * ring(y, step) + core) + h
        return owner_ref[k], slot_ref[k]

    def mine(step, h, half):
        owner, slot = block(step, h)
        rows = pl.ds(half * (BLK // 2), BLK // 2)
        return jnp.where(lax.rem(owner, 2) == core, slots_ref[slot, rows], held[slot, rows])

    copies = []
    order = ((2, 0, 2, 1), (1, 1, -1, 0), (1, 0, -1, 1))
    landing = ((far.at[0], far.at[1]), (near.at[0, 1], near.at[1, 0]), (near.at[0, 0], near.at[1, 1]))
    for i in range(3):
        for j, target in enumerate((right, left)):
            copies.append(remote(packed.at[i, j], landing[i][j], send.at[2 * i + j], recv.at[2 * i + j], target))
    swap.wait_recv()
    for i in range(2):
        for j in range(2):
            step, half = order[i][2 * j], order[i][2 * j + 1]
            for h in range(2):
                packed[i, j, h] = mine(step, h, half)
            copies[2 * i + j].start()
    for j in range(2):
        step, half = order[2][2 * j], order[2][2 * j + 1]
        copies[j].wait_recv()
        for h in range(2):
            owner, _ = block(step, h)
            packed[2, j, h] = jnp.where(owner // 2 == y, mine(step, h, half), far[j, h])
        copies[4 + j].start()
    for h in range(2):
        for half in range(2):
            out_ref[h, half * (BLK // 2) : (half + 1) * (BLK // 2)] = mine(0, h, half)
    for copy in copies[2:]:
        copy.wait_recv()
    for h in range(2):
        owner, _ = block(0, h)
        for half in range(2):
            rows = slice(half * (BLK // 2), (half + 1) * (BLK // 2))
            from_left = (owner // 2 == ring(y, -1)) | ((owner // 2 == ring(y, 2)) & (half == 0))
            value = jnp.where(from_left, near[0, half, h], near[1, half, h])
            out_ref[h, rows] = jnp.where(owner // 2 == y, out_ref[h, rows], value)
    swap.wait_send()
    for copy in copies:
        copy.wait_send()


def return_blocks(owner, slot, slots):
    dma = pltpu.SemaphoreType.DMA
    half = (2, BLK // 2, BLK)
    return pl.pallas_call(
        return_kernel,
        out_shape=jax.ShapeDtypeStruct((2, BLK, BLK), BF16),
        in_specs=[pl.BlockSpec(memory_space=pltpu.SMEM)] * 2 + [pl.BlockSpec(memory_space=pltpu.VMEM)],
        out_specs=pl.BlockSpec(memory_space=pltpu.VMEM),
        scratch_shapes=[
            pltpu.VMEM(slots.shape, BF16),
            pltpu.VMEM((3, 2) + half, BF16),
            pltpu.VMEM((2,) + half, BF16),
            pltpu.VMEM((2, 2) + half, BF16),
            dma((1,)), dma((1,)), dma((6,)), dma((6,)),
        ],
        compiler_params=pltpu.CompilerParams(
            collective_id=1, has_side_effects=True, vmem_limit_bytes=40 << 20
        ),
        cost_estimate=pl.CostEstimate(flops=0, bytes_accessed=8 << 20, transcendentals=0),
        name="return_blocks",
    )(owner, slot, slots)


def body(acts, grads_out, owners, left_stats, right_stats, left_root, right_root):
    capacity = left_stats.shape[2]
    my_index = lax.axis_index("group")
    owner = owners[0, :, 0]
    position = jnp.arange(owner.shape[0], dtype=jnp.int32)
    matches = owner[:, None] == owner[None, :]
    earlier = position[None, :] < position[:, None]
    slot = jnp.sum((matches & earlier).astype(jnp.int32), axis=1)
    here = (owner[None, :] == my_index) & (slot[None, :] == jnp.arange(capacity, dtype=jnp.int32)[:, None])
    index = jnp.sum(jnp.where(here, position[None, :], 0), axis=1)
    used = jnp.sum(here.astype(jnp.int32), axis=1)

    blocks = reduce_blocks(acts, grads_out)
    left_new, right_new, slots = slots_step(index, used, blocks, left_stats, right_stats, left_root, right_root)
    update = return_blocks(owner, slot, slots)
    return (left_new, right_new, update)


def solution(mesh):
    placed = (
        P("dp", "group"),
        P("dp", "group"),
        P("dp", None, None),
        P("dp", "group", None, None, None),
        P("dp", "group", None, None, None),
        P("dp", "group", None, None, None),
        P("dp", "group", None, None, None),
    )
    return jax.shard_map(
        body,
        mesh=mesh,
        in_specs=placed,
        out_specs=(
            P("dp", "group", None, None, None),
            P("dp", "group", None, None, None),
            P(("group", "dp"), None, None),
        ),
        check_vma=False,
    )
```

time: 339 us -> 202 us (0.60)
  waiting for transfers between devices: 222 us -> 0 us
  Pallas kernels: 0 us -> 194 us
  matrix products: 52.6 us -> 0 us
  local copies, waits for them, and re-layouts: 47.6 us -> 5.68 us
  between operations: 13.9 us -> 0.68 us
    pallas_call x0 -> x3, Pallas kernels: none -> 194 us  [the longest x1 145 us: reduce_blocks(): pl.pallas_call(reduce_kernel, out_shape=jax.ShapeDtypeStruct((16, BLK, BL...]
    reduce_scatter x2 -> x0, waiting for transfers between devices: 152 us -> none  [the longest x1 110 us: body(): lax.psum_scatter(jnp.einsum('tcf,tcd->cfd', left_part, right_part, prefer...]
    all_gather x2 -> x0, waiting for transfers between devices: 69.3 us -> none  [the longest x1 49.8 us: body(): piece = lax.all_gather(summed, 'group', axis=0, tiled=True)]
    dot_general x6 -> x0, matrix products: 52.6 us -> none  [the longest x1 22 us: body(): jnp.einsum('tcf,tcd->cfd', left_part, right_part, preferred_element_type=...]
    gather x4 -> x0, local copies, waits for them, and re-layouts: 19.5 us -> none  [the longest x1 9.17 us: body(): right_part = jnp.take(in_blocks, block_ids % col_blocks, axis=1)]
    convert_element_type x1 -> x0, local copies, waits for them, and re-layouts: 11.4 us -> none  [body(): update = lax.psum_scatter(jnp.einsum('ks,sab->kab', selector(block_ids),...]
    reshape x2 -> x0, local copies, waits for them, and re-layouts: 10.6 us -> none  [the longest x1 6.45 us: body(): in_blocks = gathered.reshape(tok_rows, col_blocks, block_size)]
  transfers between devices with their start and end apart: 4 -> 0, of which waited for: 4 -> 0; matrix products, arithmetic and copies ran while one was open for 8% -> 0% of each run, Pallas kernels for 0% -> 0%
where the time goes in v1:
time: 202 us
  Pallas kernels  194 us (96%)
  local copies, waits for them, and re-layouts  5.68 us (3%)
    pallas_call x1, Pallas kernels, reduce_blocks(): pl.pallas_call(reduce_kernel, out_shape=jax.ShapeDtypeStruct((16, BLK, BL...  145 us
    pallas_call x1, Pallas kernels, return_blocks(): pl.pallas_call(return_kernel, out_shape=jax.ShapeDtypeStruct((2, BLK, BLK...  41.8 us
    pallas_call x1, Pallas kernels, slots_step(): pl.pallas_call(slot_kernel, grid_spec=pltpu.PrefetchScalarGridSpec(num_sc...  6.82 us
    unnamed x11, local copies, waits for them, and re-layouts  5.68 us

profile of v1, /device:TPU:1, one launch (start us, length us, event | category | flops | bytes accessed | tf_op | source)
XLA Modules:
  0.0 202.0 jit_solution(11354436448778974214)
XLA Ops:
  0.6 0.7 broadcast_compare_fusion
  1.3 0.9 convert_reduce_fusion.slot_ref
  2.2 0.2 convert_reduce_fusion.1
  2.4 0.0 copy-start
  2.4 145.3 %reduce_blocks.1.block_ref = bf16[16,512,512]{2,1,0:T(8,128)(2,1)} custom-call(bf16[512,512]{1,0:T(8,128)(2,1)} %acts_ref.1, bf16[512,2048]{1,0:T(8,128)(2,1)} %grads_ref.1), custom_call_target="tpu_custom_call" | custom-call | flops 8589934592 | bytes 12582912 | tf_op jit(solution)/shard_map/reduce_blocks/pallas_call | solution.py:251
  147.7 0.0 copy-done
  147.7 0.0 copy-start.1
  147.7 1.9 copy-done.1
  149.6 0.0 copy-start.2
  149.6 1.4 copy-done.2
  151.0 0.0 copy-start.3
  151.0 1.4 copy-done.3
  152.4 0.0 copy-start.4
  152.4 6.8 %slots_step.1 = (f32[1,1,3,512,512]{4,3,2,1,0:T(8,128)}, f32[1,1,3,512,512]{4,3,2,1,0:T(8,128)}, bf16[3,512,512]{2,1,0:T(8,128)(2,1)S(1)}) custom-call(s32[3]{0:T(128)S(1)} %get-tuple-element.10.index_ref, s32[3]{0:T(128)S(1)} %get-tuple-element.9.used_ref, bf16[16,512,512]{2,1,0:T(8,128)(2,1)} %reduce_blocks.1.block_ref, ...), custom_call_target="tpu_custom_call" | custom-call | tf_op jit(solution)/shard_map/slots_step/pallas_call | solution.py:298
  159.2 0.0 copy-done.4
  159.2 41.8 %return_blocks.1 = bf16[2,512,512]{2,1,0:T(8,128)(2,1)S(1)} custom-call(s32[16]{0:T(128)S(1)} %bitcast.3, s32[16]{0:T(128)S(1)} %convert_reduce_fusion.slot_ref, bf16[3,512,512]{2,1,0:T(8,128)(2,1)S(1)} %get-tuple-element.8.slots_ref), custom_call_target="tpu_custom_call" | custom-call | bytes 8388608 | tf_op jit(solution)/shard_map/return_blocks/pallas_call | solution.py:373
  201.0 1.0 copy.11
Async XLA Ops:
  2.4 145.3 %copy-start = (f32[1,1,3,512,512]{4,3,2,1,0:T(8,128)S(1)}, f32[1,1,3,512,512]{4,3,2,1,0:T(8,128)}, u32[]{:S(2)}) copy-start(f32[1,1,3,512,512]{4,3,2,1,0:T(8,128)} %ls_ref.1) | copy-start | bytes 9437188
  147.7 1.9 copy-start.1
  149.6 1.4 copy-start.2
  151.0 1.4 copy-start.3
  152.4 6.8 %copy-start.4 = (s32[1,16,1]{1,2,0:T(1,128)S(1)}, s32[1,16,1]{1,2,0:T(1,128)}, u32[]{:S(2)}) copy-start(s32[1,16,1]{1,2,0:T(1,128)} %param.9) | copy-start | bytes 196

commit v2 on v1

v2 whole, which is shorter than its diff:
```python
import functools

import jax
import jax.numpy as jnp
from jax import lax
from jax.experimental import pallas as pl
from jax.experimental.pallas import tpu as pltpu
from jax.sharding import PartitionSpec as P

MESH = pl.DeviceIdType.MESH
STAT_DECAY = 0.9
EPSILON = 1e-06
BLK = 512
HALF = BLK // 2
SIDE = 4
GROUPS = 8
CAP = 3
PER_HALF = 4
ROUNDS = 2 * PER_HALF
PART = HALF // PER_HALF
SLOTS = 3
F32 = jnp.float32
BF16 = jnp.bfloat16


def place():
    dp, group = lax.axis_index("dp"), lax.axis_index("group")
    return dp // SIDE, group // 2, lax.rem(dp, SIDE), lax.rem(group, 2)


def ring(index, step):
    return lax.rem(index + step + SIDE, SIDE)


def device(x, y, z, core):
    return (x * SIDE + z, y * 2 + core)


def remote(src, dst, send, recv, target):
    return pltpu.make_async_remote_copy(
        src_ref=src, dst_ref=dst, send_sem=send, recv_sem=recv, device_id=target, device_id_type=MESH
    )


def greet(targets):
    barrier = pltpu.get_barrier_semaphore()
    for target in targets:
        pl.semaphore_signal(barrier, inc=1, device_id=target, device_id_type=MESH)
    pl.semaphore_wait(barrier, len(targets))


def plus(*terms):
    total = terms[0].astype(F32)
    for term in terms[1:]:
        total = total + term.astype(F32)
    return total.astype(BF16)


class RingSum:
    def __init__(self, part, me, right, left, far, near, send, recv):
        self.part, self.me = part, me
        to_right = [
            (part(ring(me, 2)).at[0], far.at[0]),
            (part(ring(me, 1)).at[1], near.at[0, 1]),
            (part(ring(me, 1)).at[0], near.at[0, 0]),
        ]
        to_left = [
            (part(ring(me, 2)).at[1], far.at[1]),
            (part(ring(me, -1)).at[0], near.at[1, 0]),
            (part(ring(me, -1)).at[1], near.at[1, 1]),
        ]
        self.far, self.near = far, near
        self.copies = []
        for i in range(3):
            for j, (target, lists) in enumerate(((right, to_right), (left, to_left))):
                src, dst = lists[i]
                self.copies.append(remote(src, dst, send.at[2 * i + j], recv.at[2 * i + j], target))

    def first(self):
        for copy in self.copies[:4]:
            copy.start()

    def merge(self):
        for j, (step, half) in enumerate(((1, 0), (-1, 1))):
            self.copies[j].wait_recv()
            ref = self.part(ring(self.me, step)).at[half]
            ref[...] = plus(ref[...], self.far[j])
            self.copies[4 + j].start()

    def total(self):
        for copy in self.copies[2:]:
            copy.wait_recv()
        mine = self.part(self.me)
        return [plus(mine[half], self.near[0, half], self.near[1, half]) for half in range(2)]

    def finish(self):
        for copy in self.copies:
            copy.wait_send()


def shampoo_kernel(
    table, acts_ref, grads_ref, ls_ref, rs_ref, lr_ref, rr_ref,
    ln_ref, rn_ref, out_ref,
    grads, turned, acts, parts, far1, near1, sums, far2, near2, blocks0, blocks1,
    left_root, right_root, result0, result1, held0, held1, packed, back_far, back_near, left_stats, right_stats,
    local_sem, acts_send, acts_recv, pair_send, pair_recv,
    send1, recv1, send2, recv2, out_send, out_recv, cross_send, cross_recv,
    swap_send, swap_recv, back_send, back_recv, stats_sem,
):
    x, y, z, core = place()
    group = y * 2 + core
    partner = device(x, y, z, 1 - core)
    along_y = [device(x, ring(y, s), z, core) for s in (1, -1, 2)]
    along_x = [device(ring(x, s), y, z, core) for s in (1, -1)]
    along_z = [device(x, y, ring(z, s), core) for s in (1, -1)]
    blocks, result, held = (blocks0, blocks1), (result0, result1), (held0, held1)

    load_grads = pltpu.make_async_copy(grads_ref, grads, local_sem.at[0])
    load_acts = pltpu.make_async_copy(acts_ref, acts.at[core, y], local_sem.at[1])
    load_acts.start()
    load_grads.start()
    loads = [
        pltpu.make_async_copy(ref.at[0, 0], buffer, local_sem.at[2 + i])
        for i, (ref, buffer) in enumerate(
            ((lr_ref, left_root), (rr_ref, right_root), (ls_ref, left_stats), (rs_ref, right_stats))
        )
    ]
    greet([partner] + along_y + along_x + along_z)

    load_acts.wait()
    own = acts.at[core, y]
    acts_out = [remote(own, own, acts_send.at[i], acts_recv.at[i], along_y[i]) for i in range(3)]
    for copy in acts_out:
        copy.start()
    acts_pair = [remote(own, own, pair_send.at[0], pair_recv.at[0], partner)]
    acts_pair[0].start()
    load_grads.wait()
    for copy in loads:
        copy.start()
    for part in range(HALF // PART * 2):
        for xd in range(SIDE):
            start = xd * BLK + part * PART
            turned[part, xd * PART : (xd + 1) * PART, :] = grads[:, start : start + PART].T
    for i, s in enumerate((-1, 1, 2)):
        acts_out[i].wait_recv()
        here = acts.at[core, ring(y, s)]
        copy = remote(here, here, pair_send.at[i + 1], pair_recv.at[i + 1], partner)
        copy.start()
        acts_pair.append(copy)

    stages1, stages2, outs, crosses = {}, {}, {}, {}

    def products(r):
        p, v = r // PER_HALF, r % PER_HALF
        h, b = lax.rem(core + p, 2), r % SLOTS
        if r == PER_HALF:
            for copy in acts_pair:
                copy.wait_recv()
        for u in range(2):
            if r >= SLOTS:
                stages1[r - SLOTS, u].finish()
            left = turned[v * 2 + u]

            def step(zd, carry, u=u, left=left):
                value = jnp.dot(left, acts[h, zd], preferred_element_type=F32).astype(BF16)
                for xd in range(SIDE):
                    piece = value[xd * PART : (xd + 1) * PART]
                    if u == 0:
                        parts[b, 0, xd, zd // 2, lax.rem(zd, 2)] = piece
                    else:
                        parts[b, 1, zd, xd // 2, xd % 2] = piece
                return carry

            lax.fori_loop(0, SIDE, step, 0)
            me, (right, left_to) = ((x, along_x), (z, along_z))[u]
            stage = RingSum(
                lambda d, u=u: parts.at[b, u, d], me, right, left_to,
                far1.at[b, u], near1.at[b, u], send1.at[b, u], recv1.at[b, u],
            )
            stage.first()
            stages1[r, u] = stage

    def merge1(r):
        for u in range(2):
            stages1[r, u].merge()

    def between(r):
        b = r % SLOTS
        for u in range(2):
            if r >= SLOTS:
                stages2[r - SLOTS, u].finish()
            total = stages1[r, u].total()
            for half in range(2):
                for o in range(2):
                    for piece in range(2):
                        sums[b, u, half * 2 + o, piece] = total[half][o, piece * (PART // 2) : (piece + 1) * (PART // 2)]
            me, (right, left_to) = ((z, along_z), (x, along_x))[u]
            stage = RingSum(
                lambda d, u=u: sums.at[b, u, d], me, right, left_to,
                far2.at[b, u], near2.at[b, u], send2.at[b, u], recv2.at[b, u],
            )
            stage.first()
            stages2[r, u] = stage

    def merge2(r):
        for u in range(2):
            stages2[r, u].merge()

    def spread(r):
        p, v = r // PER_HALF, r % PER_HALF
        for u in range(2):
            total = stages2[r, u].total()
            for half in range(2):
                start = (2 * v + u) * PART + half * (PART // 2)
                blocks[p][group, start : start + PART // 2] = total[half]
        here = blocks[p].at[group, pl.ds(v * 2 * PART, 2 * PART)]
        outs[r] = [remote(here, here, out_send.at[r, i], out_recv.at[r, i], along_y[i]) for i in range(3)]
        for copy in outs[r]:
            copy.start()
        cross = remote(here, here, cross_send.at[r, 0], cross_recv.at[r, 0], partner)
        cross.start()
        crosses[r] = [cross]

    def pass_on(r):
        p, v = r // PER_HALF, r % PER_HALF
        for i, s in enumerate((-1, 1, 2)):
            outs[r][i].wait_recv()
            here = blocks[p].at[2 * ring(y, s) + core, pl.ds(v * 2 * PART, 2 * PART)]
            cross = remote(here, here, cross_send.at[r, i + 1], cross_recv.at[r, i + 1], partner)
            cross.start()
            crosses[r].append(cross)

    swaps, backs = {}, {}

    def precondition(p):
        for r in range(p * PER_HALF, (p + 1) * PER_HALF):
            for copy in crosses[r]:
                copy.wait_recv()
        if p == 0:
            for copy in loads:
                copy.wait()
        swaps[p] = []
        for j in range(CAP):
            block = blocks[p][table[32 + 6 * p + 2 * j]]
            slot = table[33 + 6 * p + 2 * j]
            shaped = jnp.dot(left_root[slot], block, preferred_element_type=F32).astype(BF16)
            product = jnp.dot(shaped, right_root[slot], preferred_element_type=F32)
            scaling = lax.rsqrt(jnp.mean(product * product) + EPSILON)
            result[p][j] = (product * scaling).astype(BF16)
            copy = remote(result[p].at[j], held[p].at[j], swap_send.at[p, j], swap_recv.at[p, j], partner)
            copy.start()
            swaps[p].append(copy)

    def mine(p, step, half):
        to = 2 * ring(y, step) + core
        owner, rank = table[16 * p + to], table[16 * p + 8 + to]
        rows = pl.ds(half * HALF, HALF)
        value = jnp.where(lax.rem(owner, 2) == core, result[p][rank, rows], held[p][rank, rows])
        return value, owner // 2

    order = (((2, 0), (2, 1)), ((1, 1), (-1, 0)), ((1, 0), (-1, 1)))

    def back_first(p):
        for copy in swaps[p]:
            copy.wait_recv()
        far, near = back_far.at[p], back_near.at[p]
        landing = ((far.at[0], far.at[1]), (near.at[0, 1], near.at[1, 0]), (near.at[0, 0], near.at[1, 1]))
        backs[p] = []
        for i in range(3):
            for j in range(2):
                backs[p].append(
                    remote(
                        packed.at[p, i, j], landing[i][j], back_send.at[p, 2 * i + j], back_recv.at[p, 2 * i + j], along_y[j]
                    )
                )
        for i in range(2):
            for j in range(2):
                packed[p, i, j] = mine(p, *order[i][j])[0]
                backs[p][2 * i + j].start()

    def back_merge(p):
        for j in range(2):
            backs[p][j].wait_recv()
            value, at = mine(p, *order[2][j])
            packed[p, 2, j] = jnp.where(at == y, value, back_far[p, j])
            backs[p][4 + j].start()

    def back_last(p):
        for copy in backs[p][2:]:
            copy.wait_recv()
        h = lax.rem(core + p, 2)
        for half in range(2):
            value, at = mine(p, 0, half)
            from_left = at == ring(y, -1)
            if half == 0:
                from_left = from_left | (at == ring(y, 2))
            value = jnp.where(at == y, value, jnp.where(from_left, back_near[p, 0, half], back_near[p, 1, half]))
            out_ref[h, half * HALF : (half + 1) * HALF] = value

    stats_out = []

    def grams(s):
        p, at, used = table[44 + 3 * s], table[45 + 3 * s], table[46 + 3 * s]
        block = jnp.where(p == 0, blocks0[at], blocks1[at])
        block = jnp.where(used > 0, block, jnp.zeros_like(block))
        left = lax.dot_general(block, block, (((1,), (1,)), ((), ())), preferred_element_type=F32)
        left_stats[s] = STAT_DECAY * left_stats[s] + (1.0 - STAT_DECAY) * left
        right = lax.dot_general(block, block, (((0,), (0,)), ((), ())), preferred_element_type=F32)
        right_stats[s] = STAT_DECAY * right_stats[s] + (1.0 - STAT_DECAY) * right
        for i, (buffer, ref) in enumerate(((left_stats, ln_ref), (right_stats, rn_ref))):
            copy = pltpu.make_async_copy(buffer.at[s], ref.at[0, 0, s], stats_sem.at[2 * s + i])
            copy.start()
            stats_out.append(copy)

    for step in range(ROUNDS + 2):
        if step < ROUNDS:
            products(step)
        if 0 <= step - 2 < ROUNDS:
            spread(step - 2)
        if 0 <= step - 1 < ROUNDS:
            between(step - 1)
        if step == PER_HALF + 2:
            precondition(0)
        if 0 <= step < ROUNDS:
            merge1(step)
        if 0 <= step - 1 < ROUNDS:
            merge2(step - 1)
        if 0 <= step - 2 < ROUNDS:
            pass_on(step - 2)
        if step == PER_HALF + 2:
            back_first(0)
        if step == PER_HALF + 3:
            back_merge(0)
    precondition(1)
    back_first(1)
    grams(0)
    grams(1)
    back_merge(1)
    grams(2)
    back_last(0)
    back_last(1)

    for copy in acts_out + acts_pair:
        copy.wait_send()
    for r in range(ROUNDS):
        if r >= ROUNDS - SLOTS:
            for u in range(2):
                stages1[r, u].finish()
                stages2[r, u].finish()
        for copy in outs[r] + crosses[r]:
            copy.wait_send()
    for p in range(2):
        for copy in swaps[p] + backs[p]:
            copy.wait_send()
    for copy in stats_out:
        copy.wait()


def body(acts, grads_out, owners, left_stats, right_stats, left_root, right_root):
    my_index = lax.axis_index("group")
    owner = owners[0, :, 0]
    position = jnp.arange(owner.shape[0], dtype=jnp.int32)
    half = (position // 2 + position) % 2
    matches = owner[:, None] == owner[None, :]
    earlier = matches & (position[None, :] < position[:, None])
    slot = jnp.sum(earlier.astype(jnp.int32), axis=1)
    rank = jnp.sum((earlier & (half[:, None] == half[None, :])).astype(jnp.int32), axis=1)
    count = jnp.arange(CAP, dtype=jnp.int32)
    entries = []
    for p in range(2):
        at = 2 * jnp.arange(GROUPS, dtype=jnp.int32) + (jnp.arange(GROUPS, dtype=jnp.int32) + p) % 2
        entries += [owner[at], rank[at]]
    for p in range(2):
        here = (owner == my_index)[None, :] & (half == p)[None, :] & (rank[None, :] == count[:, None])
        which = jnp.sum(jnp.where(here, position[None, :] // 2, 0), axis=1)
        where = jnp.sum(jnp.where(here, slot[None, :], 0), axis=1)
        entries.append(jnp.stack([which, where], axis=1).reshape(-1))
    here = (owner == my_index)[None, :] & (slot[None, :] == count[:, None])
    entries.append(
        jnp.stack(
            [
                jnp.sum(jnp.where(here, half[None, :], 0), axis=1),
                jnp.sum(jnp.where(here, position[None, :] // 2, 0), axis=1),
                jnp.sum(here.astype(jnp.int32), axis=1),
            ],
            axis=1,
        ).reshape(-1)
    )
    table = jnp.concatenate(entries)

    dma = pltpu.SemaphoreType.DMA
    piece, small = (2, PART, BLK), (PART // 2, BLK)
    square = (BLK, BLK)
    left_new, right_new, update = pl.pallas_call(
        shampoo_kernel,
        out_shape=(
            jax.ShapeDtypeStruct(left_stats.shape, F32),
            jax.ShapeDtypeStruct(right_stats.shape, F32),
            jax.ShapeDtypeStruct((2, BLK, BLK), BF16),
        ),
        in_specs=[pl.BlockSpec(memory_space=pltpu.SMEM)] + [pl.BlockSpec(memory_space=pl.ANY)] * 6,
        out_specs=(
            pl.BlockSpec(memory_space=pl.ANY),
            pl.BlockSpec(memory_space=pl.ANY),
            pl.BlockSpec(memory_space=pltpu.VMEM),
        ),
        scratch_shapes=[
            pltpu.VMEM((BLK, SIDE * BLK), BF16),
            pltpu.VMEM((2 * PER_HALF, SIDE * PART, BLK), BF16),
            pltpu.VMEM((2, SIDE) + square, BF16),
            pltpu.VMEM((SLOTS, 2, SIDE, 2) + piece, BF16),
            pltpu.VMEM((SLOTS, 2, 2) + piece, BF16),
            pltpu.VMEM((SLOTS, 2, 2, 2) + piece, BF16),
            pltpu.VMEM((SLOTS, 2, SIDE, 2) + small, BF16),
            pltpu.VMEM((SLOTS, 2, 2) + small, BF16),
            pltpu.VMEM((SLOTS, 2, 2, 2) + small, BF16),
            pltpu.VMEM((GROUPS,) + square, BF16),
            pltpu.VMEM((GROUPS,) + square, BF16),
            pltpu.VMEM((CAP,) + square, BF16),
            pltpu.VMEM((CAP,) + square, BF16),
            pltpu.VMEM((CAP,) + square, BF16),
            pltpu.VMEM((CAP,) + square, BF16),
            pltpu.VMEM((CAP,) + square, BF16),
            pltpu.VMEM((CAP,) + square, BF16),
            pltpu.VMEM((2, 3, 2, HALF, BLK), BF16),
            pltpu.VMEM((2, 2, HALF, BLK), BF16),
            pltpu.VMEM((2, 2, 2, HALF, BLK), BF16),
            pltpu.VMEM((CAP,) + square, F32),
            pltpu.VMEM((CAP,) + square, F32),
            dma((6,)),
            dma((3,)), dma((3,)), dma((4,)), dma((4,)),
            dma((SLOTS, 2, 6)), dma((SLOTS, 2, 6)),
            dma((SLOTS, 2, 6)), dma((SLOTS, 2, 6)),
            dma((ROUNDS, 3)), dma((ROUNDS, 3)),
            dma((ROUNDS, 4)), dma((ROUNDS, 4)),
            dma((2, CAP)), dma((2, CAP)),
            dma((2, 6)), dma((2, 6)),
            dma((2 * CAP,)),
        ],
        compiler_params=pltpu.CompilerParams(
            collective_id=0, has_side_effects=True, vmem_limit_bytes=62 << 20
        ),
        cost_estimate=pl.CostEstimate(flops=12 << 30, bytes_accessed=20 << 20, transcendentals=0),
        name="shampoo",
    )(table, acts, grads_out, left_stats, right_stats, left_root, right_root)
    return (left_new, right_new, update)


def solution(mesh):
    placed = (
        P("dp", "group"),
        P("dp", "group"),
        P("dp", None, None),
        P("dp", "group", None, None, None),
        P("dp", "group", None, None, None),
        P("dp", "group", None, None, None),
        P("dp", "group", None, None, None),
    )
    return jax.shard_map(
        body,
        mesh=mesh,
        in_specs=placed,
        out_specs=(
            P("dp", "group", None, None, None),
            P("dp", "group", None, None, None),
            P(("group", "dp"), None, None),
        ),
        check_vma=False,
    )
```

time: 202 us -> 190 us (0.941)
  Pallas kernels: 194 us -> 174 us
  local copies, waits for them, and re-layouts: 5.68 us -> 12 us
    pallas_call x3 -> x1, Pallas kernels: 194 us -> 174 us  [body(): pl.pallas_call(shampoo_kernel, out_shape=(jax.ShapeDtypeStruct(left_stats...]
    gather x0 -> x4, local copies, waits for them, and re-layouts: none -> 3.9 us  [body(): entries += [owner[at], rank[at]]]
    unnamed x11 -> x7, local copies, waits for them, and re-layouts: 5.68 us -> 6.95 us
where the time goes in v2:
time: 190 us; the launch traced here: 189 us
  Pallas kernels  174 us (92%)
  local copies, waits for them, and re-layouts  12 us (6%)
    pallas_call x1, Pallas kernels, body(): pl.pallas_call(shampoo_kernel, out_shape=(jax.ShapeDtypeStruct(left_stats...  174 us
    unnamed x7, local copies, waits for them, and re-layouts  6.95 us
    gather x4, local copies, waits for them, and re-layouts, body(): entries += [owner[at], rank[at]]  3.9 us

profile of v2, /device:TPU:1, one launch (start us, length us, event | category | flops | bytes accessed | tf_op | source)
XLA Modules:
  0.0 188.8 jit_solution(1001687359446857077)
XLA Ops:
  0.7 0.7 compare_and_fusion.1
  1.3 0.9 convert_reduce_fusion
  2.3 0.2 select_reduce_fusion.3
  2.5 0.1 copy.17
  2.6 0.1 reshape.213
  2.7 0.1 copy.16
  2.8 0.1 reshape.212
  2.9 0.1 copy.18
  3.0 0.1 reshape.214
  3.1 0.6 gather_fusion.1
  3.7 1.3 gather_fusion
  5.0 0.6 gather_fusion.3
  5.7 1.3 gather_fusion.2
  7.0 0.6 concatenate.3.table
  7.6 174.2 %shampoo.1 = (f32[1,1,3,512,512]{4,3,2,1,0:T(8,128)}, f32[1,1,3,512,512]{4,3,2,1,0:T(8,128)}, bf16[2,512,512]{2,1,0:T(8,128)(2,1)}) custom-call(s32[53]{0:T(128)} %concatenate.3.table, bf16[512,512]{1,0:T(8,128)(2,1)} %acts_ref.1, bf16[512,2048]{1,0:T(8,128)(2,1)} %grads_ref.1, f32[1,1,3,512,512]{4,3,2,1,0:T(8,128)} %ls_ref.1, ...), custom_call_target="tpu_custom_call" | custom-call | flops 12884901888 | bytes 20971520 | tf_op jit(solution)/shard_map/shampoo/pallas_call | solution.py:394
  181.8 0.0 copy-start
  181.8 4.0 %copy.22 = f32[1,1,3,512,512]{4,3,2,1,0:T(8,128)} copy(f32[1,1,3,512,512]{4,3,2,1,0:T(8,128)} %get-tuple-element.22) | data formatting | bytes 6291456
  185.8 0.0 copy-done
  185.9 0.0 copy-start.1
  185.9 1.7 copy.23
  187.5 0.3 copy-done.1
  187.8 1.0 copy.24
  (9 shorter events, 0.1 us)
Async XLA Ops:
  181.8 4.0 %copy-start = (f32[1,1,3,512,512]{4,3,2,1,0:T(8,128)S(1)}, f32[1,1,3,512,512]{4,3,2,1,0:T(8,128)}, u32[]{:S(2)}) copy-start(f32[1,1,3,512,512]{4,3,2,1,0:T(8,128)} %get-tuple-element.23) | copy-start | bytes 9437188
  185.9 2.0 %copy-start.1 = (bf16[2,512,512]{2,1,0:T(8,128)(2,1)S(1)}, bf16[2,512,512]{2,1,0:T(8,128)(2,1)}, u32[]{:S(2)}) copy-start(bf16[2,512,512]{2,1,0:T(8,128)(2,1)} %get-tuple-element.24) | copy-start | bytes 3145732

commit v3 on v0

v3 whole, which is shorter than its diff:
```python
import functools

import jax
import jax.numpy as jnp
from jax import lax
from jax.experimental import pallas as pl
from jax.experimental.pallas import tpu as pltpu
from jax.sharding import PartitionSpec as P

MESH = pl.DeviceIdType.MESH
STAT_DECAY = 0.9
EPSILON = 1e-06
BLK = 512
HALF = BLK // 2
SIDE = 4
GROUPS = 8
CAP = 3
PER_HALF = 4
ROUNDS = 2 * PER_HALF
PART = HALF // PER_HALF
SLOTS = 3
F32 = jnp.float32
BF16 = jnp.bfloat16


def place():
    dp, group = lax.axis_index("dp"), lax.axis_index("group")
    return dp // SIDE, group // 2, lax.rem(dp, SIDE), lax.rem(group, 2)


def ring(index, step):
    return lax.rem(index + step + SIDE, SIDE)


def device(x, y, z, core):
    return (x * SIDE + z, y * 2 + core)


def remote(src, dst, send, recv, target):
    return pltpu.make_async_remote_copy(
        src_ref=src, dst_ref=dst, send_sem=send, recv_sem=recv, device_id=target, device_id_type=MESH
    )


def greet(targets):
    barrier = pltpu.get_barrier_semaphore()
    for target in targets:
        pl.semaphore_signal(barrier, inc=1, device_id=target, device_id_type=MESH)
    pl.semaphore_wait(barrier, len(targets))


def plus(*terms):
    total = terms[0].astype(F32)
    for term in terms[1:]:
        total = total + term.astype(F32)
    return total.astype(BF16)


class RingSum:
    def __init__(self, part, me, right, left, far, near, send, recv):
        self.part, self.me = part, me
        to_right = [
            (part(ring(me, 2)).at[0], far.at[0]),
            (part(ring(me, 1)).at[1], near.at[0, 1]),
            (part(ring(me, 1)).at[0], near.at[0, 0]),
        ]
        to_left = [
            (part(ring(me, 2)).at[1], far.at[1]),
            (part(ring(me, -1)).at[0], near.at[1, 0]),
            (part(ring(me, -1)).at[1], near.at[1, 1]),
        ]
        self.far, self.near = far, near
        self.copies = []
        for i in range(3):
            for j, (target, lists) in enumerate(((right, to_right), (left, to_left))):
                src, dst = lists[i]
                self.copies.append(remote(src, dst, send.at[2 * i + j], recv.at[2 * i + j], target))

    def first(self):
        for copy in self.copies[:4]:
            copy.start()

    def merge(self):
        for j, (step, half) in enumerate(((1, 0), (-1, 1))):
            self.copies[j].wait_recv()
            ref = self.part(ring(self.me, step)).at[half]
            ref[...] = plus(ref[...], self.far[j])
            self.copies[4 + j].start()

    def total(self):
        for copy in self.copies[2:]:
            copy.wait_recv()
        mine = self.part(self.me)
        return [plus(mine[half], self.near[0, half], self.near[1, half]) for half in range(2)]

    def finish(self):
        for copy in self.copies:
            copy.wait_send()


def gradient_kernel(
    owners, acts_ref, grads_ref, lr_ref, rr_ref,
    owned_ref, out_ref,
    grads, turned, acts, parts, far1, near1, sums, far2, near2, blocks0, blocks1,
    roots, pair_roots, roots_packed, roots_far, roots_near, holder_roots,
    result, held, packed, back_far, back_near, owned, slot_table, rank_table,
    local_sem, pair_send, pair_recv, acts_send, acts_recv, acts_cross_send, acts_cross_recv,
    send1, recv1, send2, recv2, out_send, out_recv, cross_send, cross_recv,
    swap_send, swap_recv, back_send, back_recv, roots_swap_send, roots_swap_recv, roots_send, roots_recv, owned_sem,
):
    x, y, z, core = place()
    group = y * 2 + core
    partner = device(x, y, z, 1 - core)
    along_y = [device(x, ring(y, s), z, core) for s in (1, -1)]
    along_x = [device(ring(x, s), y, z, core) for s in (1, -1)]
    along_z = [device(x, y, ring(z, s), core) for s in (1, -1)]
    blocks = (blocks0, blocks1)
    started = []

    def go(copy):
        copy.start()
        started.append(copy)
        return copy

    load_acts = pltpu.make_async_copy(acts_ref, acts.at[core, y], local_sem.at[0])
    load_grads = pltpu.make_async_copy(grads_ref, grads, local_sem.at[1])
    load_roots = [
        pltpu.make_async_copy(ref.at[0, 0], roots.at[i], local_sem.at[2 + i]) for i, ref in enumerate((lr_ref, rr_ref))
    ]
    load_acts.start()
    load_grads.start()
    for copy in load_roots:
        copy.start()
    greet([partner] + along_y + along_x + along_z)

    load_acts.wait()
    own = acts.at[core, y]
    pair = go(remote(own, own, pair_send.at[0], pair_recv.at[0], partner))
    gathers = {}

    def rows_of(h, at, start, size):
        return acts.at[h, at, pl.ds(pl.multiple_of(core * HALF + start, 16), size)]

    def acts_first(h):
        here = rows_of(h, y, 0, HALF)
        gathers[h] = [
            go(remote(here, here, acts_send.at[h, j], acts_recv.at[h, j], along_y[j])) for j in range(2)
        ]
        gathers[h, "cross"] = []

    def acts_cross(h, i, at):
        here = rows_of(h, at, 0, HALF)
        gathers[h, "cross"].append(
            go(remote(here, here, acts_cross_send.at[h, i], acts_cross_recv.at[h, i], partner))
        )

    def acts_forward(h):
        for j in range(2):
            gathers[h][j].wait_recv()
            at = ring(y, (-1, 1)[j])
            here = rows_of(h, at, j * (HALF // 2), HALF // 2)
            gathers[h].append(
                go(remote(here, here, acts_send.at[h, 2 + j], acts_recv.at[h, 2 + j], along_y[j]))
            )
            acts_cross(h, j, at)

    def acts_last(h):
        for copy in gathers[h][2:]:
            copy.wait_recv()
        acts_cross(h, 2, ring(y, 2))

    def acts_ready(h):
        for copy in gathers[h, "cross"]:
            copy.wait_recv()

    pair.wait_recv()
    acts_first(0)

    count = 2 * GROUPS
    owner = [owners[k] for k in range(count)]
    zero, one = jnp.int32(0), jnp.int32(1)
    slot, rank = [], []
    for k in range(count):
        same = [jnp.where(owner[k2] == owner[k], one, zero) for k2 in range(k)]
        slot.append(sum(same, zero))
        rank.append(sum(same[0::2], zero))
        slot_table[k] = jnp.minimum(slot[k], CAP - 1)
        rank_table[k] = jnp.minimum(rank[k], CAP - 1)
    is_mine = [owner[k] == group for k in range(count)]

    def pick(positions, test, value):
        return sum([jnp.where(is_mine[k] & test(k), value(k), zero) for k in positions], zero)

    load_grads.wait()
    for part in range(2 * PER_HALF):
        for xd in range(SIDE):
            start = xd * BLK + part * PART
            turned[part, xd * PART : (xd + 1) * PART, :] = grads[:, start : start + PART].T
    acts_forward(0)
    for copy in load_roots:
        copy.wait()
    acts_last(0)
    roots_swap = go(remote(roots, pair_roots, roots_swap_send.at[0], roots_swap_recv.at[0], partner))

    stages1, stages2, outs, crosses = {}, {}, {}, {}

    def products(r):
        p, v = r // PER_HALF, r % PER_HALF
        b = r % SLOTS
        if v == 0:
            acts_ready(p)
        for u in range(2):
            if r >= SLOTS:
                stages1[r - SLOTS, u].finish()
            left = turned[v * 2 + u]

            def step(zd, carry, u=u, left=left):
                value = jnp.dot(left, acts[p, zd], preferred_element_type=F32).astype(BF16)
                for xd in range(SIDE):
                    piece = value[xd * PART : (xd + 1) * PART]
                    if u == 0:
                        parts[b, 0, xd, zd // 2, lax.rem(zd, 2)] = piece
                    else:
                        parts[b, 1, zd, xd // 2, xd % 2] = piece
                return carry

            lax.fori_loop(0, SIDE, step, 0)
            me, (right, left_to) = ((x, along_x), (z, along_z))[u]
            stage = RingSum(
                lambda d, u=u: parts.at[b, u, d], me, right, left_to,
                far1.at[b, u], near1.at[b, u], send1.at[b, u], recv1.at[b, u],
            )
            stage.first()
            stages1[r, u] = stage

    def merge1(r):
        for u in range(2):
            stages1[r, u].merge()

    def between(r):
        b = r % SLOTS
        for u in range(2):
            if r >= SLOTS:
                stages2[r - SLOTS, u].finish()
            total = stages1[r, u].total()
            for half in range(2):
                for o in range(2):
                    for piece in range(2):
                        sums[b, u, half * 2 + o, piece] = total[half][o, piece * (PART // 2) : (piece + 1) * (PART // 2)]
            me, (right, left_to) = ((z, along_z), (x, along_x))[u]
            stage = RingSum(
                lambda d, u=u: sums.at[b, u, d], me, right, left_to,
                far2.at[b, u], near2.at[b, u], send2.at[b, u], recv2.at[b, u],
            )
            stage.first()
            stages2[r, u] = stage

    def merge2(r):
        for u in range(2):
            stages2[r, u].merge()

    def strip(r, at, start, size):
        return blocks[r // PER_HALF].at[at, pl.ds((r % PER_HALF) * 2 * PART + start, size)]

    def cross(r, i, at):
        here = strip(r, at, 0, 2 * PART)
        crosses[r].append(go(remote(here, here, cross_send.at[r, i], cross_recv.at[r, i], partner)))

    def spread(r):
        p, v = r // PER_HALF, r % PER_HALF
        for u in range(2):
            total = stages2[r, u].total()
            for half in range(2):
                start = (2 * v + u) * PART + half * (PART // 2)
                blocks[p][group, start : start + PART // 2] = total[half]
        here = strip(r, group, 0, 2 * PART)
        outs[r] = [go(remote(here, here, out_send.at[r, j], out_recv.at[r, j], along_y[j])) for j in range(2)]
        crosses[r] = []
        cross(r, 0, group)

    def pass_on(r):
        for j in range(2):
            outs[r][j].wait_recv()
            at = 2 * ring(y, (-1, 1)[j]) + core
            here = strip(r, at, j * PART, PART)
            outs[r].append(go(remote(here, here, out_send.at[r, 2 + j], out_recv.at[r, 2 + j], along_y[j])))
            cross(r, 1 + j, at)

    def pass_last(r):
        for copy in outs[r][2:]:
            copy.wait_recv()
        cross(r, 3, 2 * ring(y, 2) + core)

    def blocks_ready(p):
        for r in range(p * PER_HALF, (p + 1) * PER_HALF):
            for copy in crosses[r]:
                copy.wait_recv()

    def condition(left_root, block, right_root):
        shaped = jnp.dot(left_root, block, preferred_element_type=F32).astype(BF16)
        product = jnp.dot(shaped, right_root, preferred_element_type=F32)
        scaling = lax.rsqrt(jnp.mean(product * product) + EPSILON)
        return (product * scaling).astype(BF16)

    swaps = []

    def precondition():
        for j in range(CAP):
            def test(k, j=j):
                return rank[k] == j

            even = range(0, count, 2)
            which, at = pick(even, test, lambda k: jnp.int32(k // 2)), pick(even, test, lambda k: jnp.minimum(slot[k], CAP - 1))
            result[j] = condition(roots[0, at], blocks0[which], roots[1, at])
            swaps.append(go(remote(result.at[j], held.at[j], swap_send.at[j], swap_recv.at[j], partner)))

    class Routed:
        def __init__(self, parity, table, sources, packed, far, near, send, recv):
            self.parity, self.table, self.sources = parity, table, sources
            self.packed, self.far, self.near = packed, far, near
            self.order = (((2, 0), (2, 1)), ((1, 1), (-1, 0)), ((1, 0), (-1, 1)))
            landing = ((far.at[0], far.at[1]), (near.at[0, 1], near.at[1, 0]), (near.at[0, 0], near.at[1, 1]))
            self.copies = [
                remote(packed.at[i, j], landing[i][j], send.at[2 * i + j], recv.at[2 * i + j], along_y[j])
                for i in range(3)
                for j in range(2)
            ]

        def mine(self, step, half):
            k = 2 * (2 * ring(y, step) + core) + self.parity
            owner, at = owners[k], self.table[k]
            rows = pl.ds(half * HALF, HALF)
            return [
                jnp.where(lax.rem(owner, 2) == core, here(at, rows), there(at, rows)) for here, there in self.sources
            ], owner // 2

        def first(self):
            for i in range(2):
                for j in range(2):
                    for n, value in enumerate(self.mine(*self.order[i][j])[0]):
                        self.packed[i, j, n] = value
                    go(self.copies[2 * i + j])

        def merge(self):
            for j in range(2):
                self.copies[j].wait_recv()
                values, at = self.mine(*self.order[2][j])
                for n, value in enumerate(values):
                    self.packed[2, j, n] = jnp.where(at == y, value, self.far[j, n])
                go(self.copies[4 + j])

        def last(self, store):
            for copy in self.copies[2:]:
                copy.wait_recv()
            for half in range(2):
                values, at = self.mine(0, half)
                from_left = at == ring(y, -1)
                if half == 0:
                    from_left = from_left | (at == ring(y, 2))
                for n, value in enumerate(values):
                    arrived = jnp.where(from_left, self.near[0, half, n], self.near[1, half, n])
                    store(n, half, jnp.where(at == y, value, arrived))

    back = Routed(
        0, rank_table, [(lambda at, rows: result[at, rows], lambda at, rows: held[at, rows])],
        packed, back_far, back_near, back_send, back_recv,
    )
    routed = Routed(
        1, slot_table,
        [(lambda at, rows, n=n: roots[n, at, rows], lambda at, rows, n=n: pair_roots[n, at, rows]) for n in range(2)],
        roots_packed, roots_far, roots_near, roots_send, roots_recv,
    )

    def store_roots(n, half, value):
        holder_roots[n, half * HALF : (half + 1) * HALF] = value

    def store_update(n, half, value):
        out_ref[0, half * HALF : (half + 1) * HALF] = value

    def collect(s):
        def test(k):
            return slot[k] == s

        every = range(count)
        odd = pick(every, test, lambda k: jnp.int32(k % 2))
        at = pick(every, test, lambda k: jnp.int32(k // 2))
        used = pick(every, test, lambda k: one)
        block = jnp.where(odd > 0, blocks1[at], blocks0[at])
        owned[s] = jnp.where(used > 0, block, jnp.zeros_like(block))
        copy = pltpu.make_async_copy(owned.at[s], owned_ref.at[s], owned_sem.at[s])
        copy.start()
        return copy

    half_done = PER_HALF + 2
    for step in range(ROUNDS + 2):
        if step < ROUNDS:
            products(step)
        if 0 <= step - 2 < ROUNDS:
            spread(step - 2)
        if 0 <= step - 1 < ROUNDS:
            between(step - 1)
        if 0 <= step - 3 < ROUNDS:
            pass_last(step - 3)
        if step == half_done:
            blocks_ready(0)
            precondition()
        if step < ROUNDS:
            merge1(step)
        if 0 <= step - 1 < ROUNDS:
            merge2(step - 1)
        if step == 0:
            roots_swap.wait_recv()
            routed.first()
            acts_first(1)
        if step == 1:
            acts_forward(1)
        if step == 2:
            routed.merge()
            acts_last(1)
        if step == half_done:
            for copy in swaps:
                copy.wait_recv()
            back.first()
        if step == half_done + 1:
            back.merge()
            routed.last(store_roots)
        if step == ROUNDS + 1:
            out_ref[1] = condition(holder_roots[0], blocks1[group], holder_roots[1])
        if 0 <= step - 2 < ROUNDS:
            pass_on(step - 2)
    back.last(store_update)
    pass_last(ROUNDS - 1)
    blocks_ready(1)
    kept = [collect(s) for s in range(CAP)]

    for copy in started:
        copy.wait_send()
    for r in range(ROUNDS - SLOTS, ROUNDS):
        for u in range(2):
            stages1[r, u].finish()
            stages2[r, u].finish()
    for copy in kept:
        copy.wait()


def gradient_blocks(owners, acts, grads_out, left_root, right_root):
    dma = pltpu.SemaphoreType.DMA
    piece, small, square, half = (2, PART, BLK), (PART // 2, BLK), (BLK, BLK), (HALF, BLK)
    shapes = [
        (BLK, SIDE * BLK),
        (2 * PER_HALF, SIDE * PART, BLK),
        (2, SIDE) + square,
        (SLOTS, 2, SIDE, 2) + piece,
        (SLOTS, 2, 2) + piece,
        (SLOTS, 2, 2, 2) + piece,
        (SLOTS, 2, SIDE, 2) + small,
        (SLOTS, 2, 2) + small,
        (SLOTS, 2, 2, 2) + small,
        (GROUPS,) + square,
        (GROUPS,) + square,
        (2, CAP) + square,
        (2, CAP) + square,
        (3, 2, 2) + half,
        (2, 2) + half,
        (2, 2, 2) + half,
        (2,) + square,
        (CAP,) + square,
        (CAP,) + square,
        (3, 2, 1) + half,
        (2, 1) + half,
        (2, 2, 1) + half,
        (CAP,) + square,
    ]
    semaphores = [
        (4,), (1,), (1,), (2, 4), (2, 4), (2, 3), (2, 3),
        (SLOTS, 2, 6), (SLOTS, 2, 6), (SLOTS, 2, 6), (SLOTS, 2, 6),
        (ROUNDS, 4), (ROUNDS, 4), (ROUNDS, 4), (ROUNDS, 4),
        (CAP,), (CAP,), (6,), (6,), (1,), (1,), (6,), (6,), (CAP,),
    ]
    return pl.pallas_call(
        gradient_kernel,
        out_shape=(
            jax.ShapeDtypeStruct((CAP, BLK, BLK), BF16),
            jax.ShapeDtypeStruct((2, BLK, BLK), BF16),
        ),
        in_specs=[pl.BlockSpec(memory_space=pltpu.SMEM)] + [pl.BlockSpec(memory_space=pl.ANY)] * 4,
        out_specs=(pl.BlockSpec(memory_space=pl.ANY), pl.BlockSpec(memory_space=pltpu.VMEM)),
        scratch_shapes=[pltpu.VMEM(shape, BF16) for shape in shapes]
        + [pltpu.SMEM((2 * GROUPS,), jnp.int32)] * 2
        + [dma(shape) for shape in semaphores],
        compiler_params=pltpu.CompilerParams(
            collective_id=0, has_side_effects=True, vmem_limit_bytes=62 << 20
        ),
        cost_estimate=pl.CostEstimate(flops=12 << 30, bytes_accessed=10 << 20, transcendentals=0),
        name="gradient_blocks",
    )(owners, acts, grads_out, left_root, right_root)


def grams_kernel(block_ref, ls_ref, rs_ref, ln_ref, rn_ref):
    block = block_ref[0]
    left = lax.dot_general(block, block, (((1,), (1,)), ((), ())), preferred_element_type=F32)
    ln_ref[0, 0, 0] = STAT_DECAY * ls_ref[0, 0, 0] + (1.0 - STAT_DECAY) * left
    right = lax.dot_general(block, block, (((0,), (0,)), ((), ())), preferred_element_type=F32)
    rn_ref[0, 0, 0] = STAT_DECAY * rs_ref[0, 0, 0] + (1.0 - STAT_DECAY) * right


def grams(owned, left_stats, right_stats):
    whole = pl.BlockSpec((1, 1, 1, BLK, BLK), lambda s: (0, 0, s, 0, 0))
    return pl.pallas_call(
        grams_kernel,
        grid=(CAP,),
        in_specs=[pl.BlockSpec((1, BLK, BLK), lambda s: (s, 0, 0)), whole, whole],
        out_specs=(whole, whole),
        out_shape=(
            jax.ShapeDtypeStruct(left_stats.shape, F32),
            jax.ShapeDtypeStruct(right_stats.shape, F32),
        ),
        compiler_params=pltpu.CompilerParams(vmem_limit_bytes=62 << 20),
        name="grams",
    )(owned, left_stats, right_stats)


def body(acts, grads_out, owners, left_stats, right_stats, left_root, right_root):
    owned, update = gradient_blocks(owners.reshape(-1), acts, grads_out, left_root, right_root)
    left_new, right_new = grams(owned, left_stats, right_stats)
    return (left_new, right_new, update)


def solution(mesh):
    placed = (
        P("dp", "group"),
        P("dp", "group"),
        P("dp", None, None),
        P("dp", "group", None, None, None),
        P("dp", "group", None, None, None),
        P("dp", "group", None, None, None),
        P("dp", "group", None, None, None),
    )
    return jax.shard_map(
        body,
        mesh=mesh,
        in_specs=placed,
        out_specs=(
            P("dp", "group", None, None, None),
            P("dp", "group", None, None, None),
            P(("group", "dp"), None, None),
        ),
        check_vma=False,
    )
```

time: 339 us -> 179 us (0.53)
  waiting for transfers between devices: 222 us -> 0 us
  Pallas kernels: 0 us -> 177 us
  matrix products: 52.6 us -> 0 us
  local copies, waits for them, and re-layouts: 47.6 us -> 0.97 us
  between operations: 13.9 us -> 0.65 us
    pallas_call x0 -> x2, Pallas kernels: none -> 177 us  [the longest x1 170 us: gradient_blocks(): pl.pallas_call(gradient_kernel, out_shape=(jax.ShapeDtypeStruct((CAP, BLK...]
    reduce_scatter x2 -> x0, waiting for transfers between devices: 152 us -> none  [the longest x1 110 us: body(): lax.psum_scatter(jnp.einsum('tcf,tcd->cfd', left_part, right_part, prefer...]
    all_gather x2 -> x0, waiting for transfers between devices: 69.3 us -> none  [the longest x1 49.8 us: body(): piece = lax.all_gather(summed, 'group', axis=0, tiled=True)]
    dot_general x6 -> x0, matrix products: 52.6 us -> none  [the longest x1 22 us: body(): jnp.einsum('tcf,tcd->cfd', left_part, right_part, preferred_element_type=...]
    gather x4 -> x0, local copies, waits for them, and re-layouts: 19.5 us -> none  [the longest x1 9.17 us: body(): right_part = jnp.take(in_blocks, block_ids % col_blocks, axis=1)]
    convert_element_type x1 -> x0, local copies, waits for them, and re-layouts: 11.4 us -> none  [body(): update = lax.psum_scatter(jnp.einsum('ks,sab->kab', selector(block_ids),...]
    reshape x2 -> x0, local copies, waits for them, and re-layouts: 10.6 us -> none  [the longest x1 6.45 us: body(): in_blocks = gathered.reshape(tok_rows, col_blocks, block_size)]
    unnamed x12 -> x3, local copies, waits for them, and re-layouts: 6.11 us -> 0.97 us
  transfers between devices with their start and end apart: 4 -> 0, of which waited for: 4 -> 0; matrix products, arithmetic and copies ran while one was open for 8% -> 0% of each run, Pallas kernels for 0% -> 0%
where the time goes in v3:
time: 179 us
  Pallas kernels  177 us (99%)
    pallas_call x1, Pallas kernels, gradient_blocks(): pl.pallas_call(gradient_kernel, out_shape=(jax.ShapeDtypeStruct((CAP, BLK...  170 us
    pallas_call x1, Pallas kernels, grams(): pl.pallas_call(grams_kernel, grid=(CAP,), in_specs=[pl.BlockSpec((1, BLK,...  7.34 us

profile of v3, /device:TPU:1, one launch (start us, length us, event | category | flops | bytes accessed | tf_op | source)
XLA Modules:
  0.0 178.7 jit_solution(9105600768141774719)
XLA Ops:
  0.6 169.7 %gradient_blocks.1 = (bf16[3,512,512]{2,1,0:T(8,128)(2,1)}, bf16[2,512,512]{2,1,0:T(8,128)(2,1)}) custom-call(s32[16]{0:T(128)} %bitcast.1, bf16[512,512]{1,0:T(8,128)(2,1)} %acts_ref.1, bf16[512,2048]{1,0:T(8,128)(2,1)} %grads_ref.1, bf16[1,1,3,512,512]{4,3,2,1,0:T(8,128)(2,1)} %lr_ref.1, bf16[1,1,3,512,512]{4,3,2,1,0:T(8,128)(2,1)} %rr_ref.1), custom_call_target="tpu_custom_call" | custom-call | flops 12884901888 | bytes 10485760 | tf_op jit(solution)/shard_map/gradient_blocks/pallas_call | solution.py:480
  170.4 0.0 copy-start
  170.4 7.3 %grams.1 = (f32[1,1,3,512,512]{4,3,2,1,0:T(8,128)}, f32[1,1,3,512,512]{4,3,2,1,0:T(8,128)}) custom-call(bf16[3,512,512]{2,1,0:T(8,128)(2,1)} %get-tuple-element.7.block_ref, f32[1,1,3,512,512]{4,3,2,1,0:T(8,128)} %ls_ref.1, f32[1,1,3,512,512]{4,3,2,1,0:T(8,128)} %rs_ref.1), custom_call_target="tpu_custom_call" | custom-call | tf_op jit(solution)/shard_map/grams/pallas_call | solution.py:509
  177.7 0.0 copy-done
  177.7 1.0 copy.11
Async XLA Ops:
  170.4 7.3 %copy-start = (bf16[2,512,512]{2,1,0:T(8,128)(2,1)S(1)}, bf16[2,512,512]{2,1,0:T(8,128)(2,1)}, u32[]{:S(2)}) copy-start(bf16[2,512,512]{2,1,0:T(8,128)(2,1)} %get-tuple-element.16) | copy-start | bytes 3145732

commit v4 on v3

--- a/solution.py
+++ b/solution.py
@@ -15,10 +15,15 @@
 SIDE = 4
 GROUPS = 8
 CAP = 3
-PER_HALF = 4
-ROUNDS = 2 * PER_HALF
-PART = HALF // PER_HALF
-SLOTS = 3
+QUARTER = HALF // 2
+TILE = BLK
+SIZES = (64, 64, 64, 64, 64, 64, 64, 64)
+ROUNDS = len(SIZES)
+PER_HALF = ROUNDS // 2
+LARGEST = max(SIZES)
+STARTS = [2 * sum(SIZES[r - r % PER_HALF : r]) for r in range(ROUNDS)]
+SLOTS = 4
+MERGE1, BETWEEN, MERGE2, SPREAD, PASS_ON, PASS_LAST = 0, 1, 1, 2, 2, 3
 F32 = jnp.float32
 BF16 = jnp.bfloat16
 
@@ -142,10 +147,12 @@
         return acts.at[h, at, pl.ds(pl.multiple_of(core * HALF + start, 16), size)]
 
     def acts_first(h):
-        here = rows_of(h, y, 0, HALF)
-        gathers[h] = [
-            go(remote(here, here, acts_send.at[h, j], acts_recv.at[h, j], along_y[j])) for j in range(2)
-        ]
+        gathers[h] = []
+        for i in range(2):
+            for j in range(2):
+                here = rows_of(h, y, (i ^ j) * QUARTER, QUARTER)
+                n = 2 * i + j
+                gathers[h].append(go(remote(here, here, acts_send.at[h, n], acts_recv.at[h, n], along_y[j])))
         gathers[h, "cross"] = []
 
     def acts_cross(h, i, at):
@@ -157,15 +164,15 @@
     def acts_forward(h):
         for j in range(2):
             gathers[h][j].wait_recv()
-            at = ring(y, (-1, 1)[j])
-            here = rows_of(h, at, j * (HALF // 2), HALF // 2)
-            gathers[h].append(
-                go(remote(here, here, acts_send.at[h, 2 + j], acts_recv.at[h, 2 + j], along_y[j]))
-            )
-            acts_cross(h, j, at)
+            here = rows_of(h, ring(y, (-1, 1)[j]), j * QUARTER, QUARTER)
+            n = 4 + j
+            gathers[h].append(go(remote(here, here, acts_send.at[h, n], acts_recv.at[h, n], along_y[j])))
+        for j in range(2):
+            gathers[h][2 + j].wait_recv()
+            acts_cross(h, j, ring(y, (-1, 1)[j]))
 
     def acts_last(h):
-        for copy in gathers[h][2:]:
+        for copy in gathers[h][4:]:
             copy.wait_recv()
         acts_cross(h, 2, ring(y, 2))
 
@@ -192,10 +199,9 @@
         return sum([jnp.where(is_mine[k] & test(k), value(k), zero) for k in positions], zero)
 
     load_grads.wait()
-    for part in range(2 * PER_HALF):
-        for xd in range(SIDE):
-            start = xd * BLK + part * PART
-            turned[part, xd * PART : (xd + 1) * PART, :] = grads[:, start : start + PART].T
+    for xd in range(SIDE):
+        for start in range(0, BLK, QUARTER):
+            turned[xd, start : start + QUARTER, :] = grads[:, xd * BLK + start : xd * BLK + start + QUARTER].T
     acts_forward(0)
     for copy in load_roots:
         copy.wait()
@@ -205,30 +211,30 @@
     stages1, stages2, outs, crosses = {}, {}, {}, {}
 
     def products(r):
-        p, v = r // PER_HALF, r % PER_HALF
-        b = r % SLOTS
-        if v == 0:
+        p, b, size = r // PER_HALF, r % SLOTS, SIZES[r]
+        if r % PER_HALF == 0:
             acts_ready(p)
         for u in range(2):
             if r >= SLOTS:
                 stages1[r - SLOTS, u].finish()
-            left = turned[v * 2 + u]
+            left = turned[:, STARTS[r] + u * size : STARTS[r] + (u + 1) * size, :].reshape(SIDE * size, BLK)
 
             def step(zd, carry, u=u, left=left):
                 value = jnp.dot(left, acts[p, zd], preferred_element_type=F32).astype(BF16)
                 for xd in range(SIDE):
-                    piece = value[xd * PART : (xd + 1) * PART]
+                    piece = value[xd * size : (xd + 1) * size]
                     if u == 0:
-                        parts[b, 0, xd, zd // 2, lax.rem(zd, 2)] = piece
+                        parts[b, 0, xd, zd // 2, lax.rem(zd, 2), 0:size] = piece
                     else:
-                        parts[b, 1, zd, xd // 2, xd % 2] = piece
+                        parts[b, 1, zd, xd // 2, xd % 2, 0:size] = piece
                 return carry
 
             lax.fori_loop(0, SIDE, step, 0)
             me, (right, left_to) = ((x, along_x), (z, along_z))[u]
+            rows = pl.ds(0, size)
             stage = RingSum(
-                lambda d, u=u: parts.at[b, u, d], me, right, left_to,
-                far1.at[b, u], near1.at[b, u], send1.at[b, u], recv1.at[b, u],
+                lambda d, u=u: parts.at[b, u, d, :, :, rows], me, right, left_to,
+                far1.at[b, u, :, :, rows], near1.at[b, u, :, :, :, rows], send1.at[b, u], recv1.at[b, u],
             )
             stage.first()
             stages1[r, u] = stage
@@ -238,7 +244,7 @@
             stages1[r, u].merge()
 
     def between(r):
-        b = r % SLOTS
+        b, size = r % SLOTS, SIZES[r] // 2
         for u in range(2):
             if r >= SLOTS:
                 stages2[r - SLOTS, u].finish()
@@ -246,11 +252,12 @@
             for half in range(2):
                 for o in range(2):
                     for piece in range(2):
-                        sums[b, u, half * 2 + o, piece] = total[half][o, piece * (PART // 2) : (piece + 1) * (PART // 2)]
+                        sums[b, u, half * 2 + o, piece, 0:size] = total[half][o, piece * size : (piece + 1) * size]
             me, (right, left_to) = ((z, along_z), (x, along_x))[u]
+            rows = pl.ds(0, size)
             stage = RingSum(
-                lambda d, u=u: sums.at[b, u, d], me, right, left_to,
-                far2.at[b, u], near2.at[b, u], send2.at[b, u], recv2.at[b, u],
+                lambda d, u=u: sums.at[b, u, d, :, rows], me, right, left_to,
+                far2.at[b, u, :, rows], near2.at[b, u, :, :, rows], send2.at[b, u], recv2.at[b, u],
             )
             stage.first()
             stages2[r, u] = stage
@@ -260,34 +267,37 @@
             stages2[r, u].merge()
 
     def strip(r, at, start, size):
-        return blocks[r // PER_HALF].at[at, pl.ds((r % PER_HALF) * 2 * PART + start, size)]
+        return blocks[r // PER_HALF].at[at, pl.ds(STARTS[r] + start, size)]
 
     def cross(r, i, at):
-        here = strip(r, at, 0, 2 * PART)
+        here = strip(r, at, 0, 2 * SIZES[r])
         crosses[r].append(go(remote(here, here, cross_send.at[r, i], cross_recv.at[r, i], partner)))
 
     def spread(r):
-        p, v = r // PER_HALF, r % PER_HALF
+        p, size = r // PER_HALF, SIZES[r]
         for u in range(2):
             total = stages2[r, u].total()
             for half in range(2):
-                start = (2 * v + u) * PART + half * (PART // 2)
-                blocks[p][group, start : start + PART // 2] = total[half]
-        here = strip(r, group, 0, 2 * PART)
-        outs[r] = [go(remote(here, here, out_send.at[r, j], out_recv.at[r, j], along_y[j])) for j in range(2)]
-        crosses[r] = []
+                start = STARTS[r] + u * size + half * (size // 2)
+                blocks[p][group, start : start + size // 2] = total[half]
+        outs[r], crosses[r] = [], []
+        for i in range(2):
+            for j in range(2):
+                here, n = strip(r, group, (i ^ j) * size, size), 2 * i + j
+                outs[r].append(go(remote(here, here, out_send.at[r, n], out_recv.at[r, n], along_y[j])))
         cross(r, 0, group)
 
     def pass_on(r):
         for j in range(2):
             outs[r][j].wait_recv()
-            at = 2 * ring(y, (-1, 1)[j]) + core
-            here = strip(r, at, j * PART, PART)
-            outs[r].append(go(remote(here, here, out_send.at[r, 2 + j], out_recv.at[r, 2 + j], along_y[j])))
-            cross(r, 1 + j, at)
+            here, n = strip(r, 2 * ring(y, (-1, 1)[j]) + core, j * SIZES[r], SIZES[r]), 4 + j
+            outs[r].append(go(remote(here, here, out_send.at[r, n], out_recv.at[r, n], along_y[j])))
+        for j in range(2):
+            outs[r][2 + j].wait_recv()
+            cross(r, 1 + j, 2 * ring(y, (-1, 1)[j]) + core)
 
     def pass_last(r):
-        for copy in outs[r][2:]:
+        for copy in outs[r][4:]:
             copy.wait_recv()
         cross(r, 3, 2 * ring(y, 2) + core)
 
@@ -334,12 +344,11 @@
                 jnp.where(lax.rem(owner, 2) == core, here(at, rows), there(at, rows)) for here, there in self.sources
             ], owner // 2
 
-        def first(self):
-            for i in range(2):
-                for j in range(2):
-                    for n, value in enumerate(self.mine(*self.order[i][j])[0]):
-                        self.packed[i, j, n] = value
-                    go(self.copies[2 * i + j])
+        def send(self, i):
+            for j in range(2):
+                for n, value in enumerate(self.mine(*self.order[i][j])[0]):
+                    self.packed[i, j, n] = value
+                go(self.copies[2 * i + j])
 
         def merge(self):
             for j in range(2):
@@ -365,14 +374,17 @@
         0, rank_table, [(lambda at, rows: result[at, rows], lambda at, rows: held[at, rows])],
         packed, back_far, back_near, back_send, back_recv,
     )
-    routed = Routed(
-        1, slot_table,
-        [(lambda at, rows, n=n: roots[n, at, rows], lambda at, rows, n=n: pair_roots[n, at, rows]) for n in range(2)],
-        roots_packed, roots_far, roots_near, roots_send, roots_recv,
-    )
-
-    def store_roots(n, half, value):
-        holder_roots[n, half * HALF : (half + 1) * HALF] = value
+    routed = [
+        Routed(
+            1, slot_table,
+            [(lambda at, rows, n=n: roots[n, at, rows], lambda at, rows, n=n: pair_roots[n, at, rows])],
+            roots_packed.at[n], roots_far.at[n], roots_near.at[n], roots_send.at[n], roots_recv.at[n],
+        )
+        for n in range(2)
+    ]
+
+    def store_roots(side, _, half, value):
+        holder_roots[side, half * HALF : (half + 1) * HALF] = value
 
     def store_update(n, half, value):
         out_ref[0, half * HALF : (half + 1) * HALF] = value
@@ -391,45 +403,52 @@
         copy.start()
         return copy
 
-    half_done = PER_HALF + 2
-    for step in range(ROUNDS + 2):
-        if step < ROUNDS:
-            products(step)
-        if 0 <= step - 2 < ROUNDS:
-            spread(step - 2)
-        if 0 <= step - 1 < ROUNDS:
-            between(step - 1)
-        if 0 <= step - 3 < ROUNDS:
-            pass_last(step - 3)
+    half_done = PER_HALF - 1 + PASS_LAST
+
+    def at_lag(part, lag):
+        if 0 <= step - lag < ROUNDS:
+            part(step - lag)
+
+    for step in range(ROUNDS + PASS_LAST):
+        at_lag(products, 0)
+        at_lag(spread, SPREAD)
+        at_lag(pass_last, PASS_LAST)
+        at_lag(between, BETWEEN)
         if step == half_done:
             blocks_ready(0)
             precondition()
-        if step < ROUNDS:
-            merge1(step)
-        if 0 <= step - 1 < ROUNDS:
-            merge2(step - 1)
+        at_lag(merge1, MERGE1)
+        at_lag(merge2, MERGE2)
+        if step == ROUNDS - 1 + SPREAD:
+            out_ref[1] = condition(holder_roots[0], blocks1[group], holder_roots[1])
+        at_lag(pass_on, PASS_ON)
         if step == 0:
+            acts_first(1)
             roots_swap.wait_recv()
-            routed.first()
-            acts_first(1)
+            routed[0].send(0)
         if step == 1:
             acts_forward(1)
+            routed[0].send(1)
         if step == 2:
-            routed.merge()
             acts_last(1)
+            routed[0].merge()
+        if step == 3:
+            routed[1].send(0)
+        if step == 4:
+            routed[1].send(1)
+        if step == 5:
+            routed[1].merge()
         if step == half_done:
             for copy in swaps:
                 copy.wait_recv()
-            back.first()
+            back.send(0)
+            back.send(1)
+        if step == ROUNDS - 1:
+            for n in range(2):
+                routed[n].last(functools.partial(store_roots, n))
         if step == half_done + 1:
             back.merge()
-            routed.last(store_roots)
-        if step == ROUNDS + 1:
-            out_ref[1] = condition(holder_roots[0], blocks1[group], holder_roots[1])
-        if 0 <= step - 2 < ROUNDS:
-            pass_on(step - 2)
     back.last(store_update)
-    pass_last(ROUNDS - 1)
     blocks_ready(1)
     kept = [collect(s) for s in range(CAP)]
 
@@ -445,10 +464,10 @@
 
 def gradient_blocks(owners, acts, grads_out, left_root, right_root):
     dma = pltpu.SemaphoreType.DMA
-    piece, small, square, half = (2, PART, BLK), (PART // 2, BLK), (BLK, BLK), (HALF, BLK)
+    piece, small, square, half = (2, LARGEST, BLK), (LARGEST // 2, BLK), (BLK, BLK), (HALF, BLK)
     shapes = [
         (BLK, SIDE * BLK),
-        (2 * PER_HALF, SIDE * PART, BLK),
+        (SIDE,) + square,
         (2, SIDE) + square,
         (SLOTS, 2, SIDE, 2) + piece,
         (SLOTS, 2, 2) + piece,
@@ -460,9 +479,9 @@
         (GROUPS,) + square,
         (2, CAP) + square,
         (2, CAP) + square,
-        (3, 2, 2) + half,
-        (2, 2) + half,
-        (2, 2, 2) + half,
+        (2, 3, 2, 1) + half,
+        (2, 2, 1) + half,
+        (2, 2, 2, 1) + half,
         (2,) + square,
         (CAP,) + square,
         (CAP,) + square,
@@ -472,10 +491,10 @@
         (CAP,) + square,
     ]
     semaphores = [
-        (4,), (1,), (1,), (2, 4), (2, 4), (2, 3), (2, 3),
+        (4,), (1,), (1,), (2, 6), (2, 6), (2, 3), (2, 3),
         (SLOTS, 2, 6), (SLOTS, 2, 6), (SLOTS, 2, 6), (SLOTS, 2, 6),
-        (ROUNDS, 4), (ROUNDS, 4), (ROUNDS, 4), (ROUNDS, 4),
-        (CAP,), (CAP,), (6,), (6,), (1,), (1,), (6,), (6,), (CAP,),
+        (ROUNDS, 6), (ROUNDS, 6), (ROUNDS, 4), (ROUNDS, 4),
+        (CAP,), (CAP,), (6,), (6,), (1,), (1,), (2, 6), (2, 6), (CAP,),
     ]
     return pl.pallas_call(
         gradient_kernel,
@@ -498,19 +517,20 @@
 
 def grams_kernel(block_ref, ls_ref, rs_ref, ln_ref, rn_ref):
     block = block_ref[0]
-    left = lax.dot_general(block, block, (((1,), (1,)), ((), ())), preferred_element_type=F32)
+    rows = pl.ds(pl.multiple_of(pl.program_id(1) * TILE, TILE), TILE)
+    left = lax.dot_general(block_ref[0, rows], block, (((1,), (1,)), ((), ())), preferred_element_type=F32)
     ln_ref[0, 0, 0] = STAT_DECAY * ls_ref[0, 0, 0] + (1.0 - STAT_DECAY) * left
-    right = lax.dot_general(block, block, (((0,), (0,)), ((), ())), preferred_element_type=F32)
+    right = lax.dot_general(block_ref[0, :, rows], block, (((0,), (0,)), ((), ())), preferred_element_type=F32)
     rn_ref[0, 0, 0] = STAT_DECAY * rs_ref[0, 0, 0] + (1.0 - STAT_DECAY) * right
 
 
 def grams(owned, left_stats, right_stats):
-    whole = pl.BlockSpec((1, 1, 1, BLK, BLK), lambda s: (0, 0, s, 0, 0))
+    part = pl.BlockSpec((1, 1, 1, TILE, BLK), lambda s, i: (0, 0, s, i, 0))
     return pl.pallas_call(
         grams_kernel,
-        grid=(CAP,),
-        in_specs=[pl.BlockSpec((1, BLK, BLK), lambda s: (s, 0, 0)), whole, whole],
-        out_specs=(whole, whole),
+        grid=(CAP, BLK // TILE),
+        in_specs=[pl.BlockSpec((1, BLK, BLK), lambda s, i: (s, 0, 0)), part, part],
+        out_specs=(part, part),
         out_shape=(
             jax.ShapeDtypeStruct(left_stats.shape, F32),
             jax.ShapeDtypeStruct(right_stats.shape, F32),

time: 179 us -> 152 us (0.85)
  Pallas kernels: 177 us -> 150 us
    pallas_call x1, Pallas kernels: 170 us -> 143 us  [gradient_blocks(): pl.pallas_call(gradient_kernel, out_shape=(jax.ShapeDtypeStruct((CAP, BLK...]
where the time goes in v4:
time: 152 us
  Pallas kernels  150 us (99%)
    pallas_call x1, Pallas kernels, gradient_blocks(): pl.pallas_call(gradient_kernel, out_shape=(jax.ShapeDtypeStruct((CAP, BLK...  143 us
    pallas_call x1, Pallas kernels, grams(): pl.pallas_call(grams_kernel, grid=(CAP, BLK // TILE), in_specs=[pl.BlockS...  7.35 us

profile of v4, /device:TPU:1, one launch (start us, length us, event | category | flops | bytes accessed | tf_op | source)
XLA Modules:
  0.0 151.9 jit_solution(18098513862443341080)
XLA Ops:
  0.6 142.9 %gradient_blocks.1 = (bf16[3,512,512]{2,1,0:T(8,128)(2,1)}, bf16[2,512,512]{2,1,0:T(8,128)(2,1)}) custom-call(s32[16]{0:T(128)} %bitcast.1, bf16[512,512]{1,0:T(8,128)(2,1)} %acts_ref.1, bf16[512,2048]{1,0:T(8,128)(2,1)} %grads_ref.1, bf16[1,1,3,512,512]{4,3,2,1,0:T(8,128)(2,1)} %lr_ref.1, bf16[1,1,3,512,512]{4,3,2,1,0:T(8,128)(2,1)} %rr_ref.1), custom_call_target="tpu_custom_call" | custom-call | flops 12884901888 | bytes 10485760 | tf_op jit(solution)/shard_map/gradient_blocks/pallas_call | solution.py:499
  143.6 0.0 copy-start
  143.6 7.3 %grams.1 = (f32[1,1,3,512,512]{4,3,2,1,0:T(8,128)}, f32[1,1,3,512,512]{4,3,2,1,0:T(8,128)}) custom-call(bf16[3,512,512]{2,1,0:T(8,128)(2,1)} %get-tuple-element.7.block_ref, f32[1,1,3,512,512]{4,3,2,1,0:T(8,128)} %ls_ref.1, f32[1,1,3,512,512]{4,3,2,1,0:T(8,128)} %rs_ref.1), custom_call_target="tpu_custom_call" | custom-call | tf_op jit(solution)/shard_map/grams/pallas_call | solution.py:529
  150.9 0.0 copy-done
  150.9 1.0 copy.11
Async XLA Ops:
  143.6 7.4 %copy-start = (bf16[2,512,512]{2,1,0:T(8,128)(2,1)S(1)}, bf16[2,512,512]{2,1,0:T(8,128)(2,1)}, u32[]{:S(2)}) copy-start(bf16[2,512,512]{2,1,0:T(8,128)(2,1)} %get-tuple-element.16) | copy-start | bytes 3145732

commit v5 on v4

v5 whole, which is shorter than its diff:
```python
import functools

import jax
import jax.numpy as jnp
from jax import lax
from jax.experimental import pallas as pl
from jax.experimental.pallas import tpu as pltpu
from jax.sharding import PartitionSpec as P

MESH = pl.DeviceIdType.MESH
STAT_DECAY = 0.9
EPSILON = 1e-06
BLK = 512
HALF = BLK // 2
SIDE = 4
GROUPS = 8
CAP = 3
QUARTER = HALF // 2
TILE = BLK
COLS = 128
PER_HALF = BLK // COLS
ROUNDS = 2 * PER_HALF
SLOTS = 3
F32 = jnp.float32
BF16 = jnp.bfloat16


def place():
    dp, group = lax.axis_index("dp"), lax.axis_index("group")
    return dp // SIDE, group // 2, lax.rem(dp, SIDE), lax.rem(group, 2)


def ring(index, step):
    return lax.rem(index + step + SIDE, SIDE)


def device(x, y, z, core):
    return (x * SIDE + z, y * 2 + core)


def remote(src, dst, send, recv, target):
    return pltpu.make_async_remote_copy(
        src_ref=src, dst_ref=dst, send_sem=send, recv_sem=recv, device_id=target, device_id_type=MESH
    )


def greet(targets):
    barrier = pltpu.get_barrier_semaphore()
    for target in targets:
        pl.semaphore_signal(barrier, inc=1, device_id=target, device_id_type=MESH)
    pl.semaphore_wait(barrier, len(targets))


def plus(*terms):
    total = terms[0].astype(F32)
    for term in terms[1:]:
        total = total + term.astype(F32)
    return total.astype(BF16)


class RingSum:
    def __init__(self, parts, me, right, left, far, near, send, recv):
        self.parts, self.me, self.far, self.near = parts, me, far, near

        def copy(d, half, dst, recv_sem, target):
            return remote(parts.at[ring(me, d), half], dst, send, recv_sem, target)

        self.copies = [
            copy(2, 0, far.at[0], recv.at[0], right),
            copy(2, 1, far.at[1], recv.at[1], left),
            copy(1, 1, near.at[0, 1], recv.at[2], right),
            copy(-1, 0, near.at[1, 0], recv.at[2], left),
            copy(1, 0, near.at[0, 0], recv.at[2], right),
            copy(-1, 1, near.at[1, 1], recv.at[2], left),
        ]
        sent = parts.at[pl.ds(0, SIDE - 1)]
        self.all_sent = remote(sent, sent, send, recv.at[2], right)
        self.all_near = remote(near, near, send, recv.at[2], right)

    def first(self):
        for copy in self.copies[:4]:
            copy.start()

    def merge(self):
        for j, (step, half) in enumerate(((1, 0), (-1, 1))):
            self.copies[j].wait_recv()
            at = ring(self.me, step)
            self.parts[at, half] = plus(self.parts[at, half], self.far[j])
            self.copies[4 + j].start()

    def total(self):
        self.all_near.wait_recv()
        return [plus(self.parts[self.me, half], self.near[0, half], self.near[1, half]) for half in range(2)]

    def finish(self):
        self.all_sent.wait_send()


class Routed:
    def __init__(self, parity, owners, table, y, core, along_y, here, there, packed, far, near, send, recv):
        self.parity, self.owners, self.table, self.y, self.core = parity, owners, table, y, core
        self.here, self.there, self.packed, self.far, self.near = here, there, packed, far, near
        self.order = (((2, 0), (2, 1)), ((1, 1), (-1, 0)), ((1, 0), (-1, 1)))
        landing = ((far.at[0], far.at[1]), (near.at[0, 1], near.at[1, 0]), (near.at[0, 0], near.at[1, 1]))
        self.copies = [
            remote(packed.at[i, j], landing[i][j], send, recv.at[j if i == 0 else 2], along_y[j])
            for i in range(3)
            for j in range(2)
        ]
        self.all_sent = remote(packed, packed, send, recv.at[2], along_y[0])
        self.all_near = remote(near, near, send, recv.at[2], along_y[0])

    def mine(self, step, half):
        k = 2 * (2 * ring(self.y, step) + self.core) + self.parity
        owner, at = self.owners[k], self.table[k]
        rows = pl.ds(half * HALF, HALF)
        return jnp.where(lax.rem(owner, 2) == self.core, self.here[at, rows], self.there[at, rows]), owner // 2

    def send(self, i):
        for j in range(2):
            self.packed[i, j] = self.mine(*self.order[i][j])[0]
            self.copies[2 * i + j].start()

    def merge(self):
        for j in range(2):
            self.copies[j].wait_recv()
            value, at = self.mine(*self.order[2][j])
            self.packed[2, j] = jnp.where(at == self.y, value, self.far[j])
            self.copies[4 + j].start()

    def last(self, out):
        self.all_near.wait_recv()
        for half in range(2):
            value, at = self.mine(0, half)
            from_left = at == ring(self.y, -1)
            if half == 0:
                from_left = from_left | (at == ring(self.y, 2))
            arrived = jnp.where(from_left, self.near[0, half], self.near[1, half])
            out[half * HALF : (half + 1) * HALF] = jnp.where(at == self.y, value, arrived)

    def finish(self):
        self.all_sent.wait_send()


def gradient_kernel(
    owners, acts_ref, grads_ref, lr_ref, rr_ref,
    owned_ref, out_ref,
    grads, turned, acts, parts, far1, near1, sums, far2, near2, blocks0, blocks1,
    roots, pair_roots, roots_packed, roots_far, roots_near, holder_roots, owned, slot_table,
    local_sem, pair_send, pair_recv, acts_send, acts_recv, acts_cross_send, acts_cross_recv,
    send1, recv1, send2, recv2, out_send, out_recv, cross_send, cross_recv,
    roots_swap_send, roots_swap_recv, roots_send, roots_recv, owned_sem,
):
    x, y, z, core = place()
    group = y * 2 + core
    partner = device(x, y, z, 1 - core)
    along_y = [device(x, ring(y, s), z, core) for s in (1, -1)]
    along_x = [device(ring(x, s), y, z, core) for s in (1, -1)]
    along_z = [device(x, y, ring(z, s), core) for s in (1, -1)]
    blocks = (blocks0, blocks1)
    started = []

    def go(copy):
        copy.start()
        started.append(copy)
        return copy

    load_acts = [
        pltpu.make_async_copy(acts_ref.at[:, pl.ds(v * COLS, COLS)], acts.at[core, v, y], local_sem.at[v])
        for v in range(PER_HALF)
    ]
    load_grads = pltpu.make_async_copy(grads_ref, grads, local_sem.at[PER_HALF])
    load_roots = [
        pltpu.make_async_copy(ref.at[0, 0], roots.at[i], local_sem.at[PER_HALF + 1 + i])
        for i, ref in enumerate((lr_ref, rr_ref))
    ]
    for copy in load_acts + [load_grads] + load_roots:
        copy.start()
    greet([partner] + along_y + along_x + along_z)

    for copy in load_acts:
        copy.wait()
    own = acts.at[core, :, y]
    pair = go(remote(own, own, pair_send.at[0], pair_recv.at[0], partner))
    spans = ((0, 0, 1), (0, 1, PER_HALF - 1), (1, 0, PER_HALF))
    gathers, gather_crosses = {}, {}

    def tokens(g, at, start, size):
        h, first, number = spans[g]
        return acts.at[h, pl.ds(first, number), at, pl.ds(pl.multiple_of(core * HALF + start, 16), size)]

    def acts_first(g):
        gathers[g], gather_crosses[g] = [], []
        for i in range(2):
            for j in range(2):
                here, n = tokens(g, y, (i ^ j) * QUARTER, QUARTER), 2 * i + j
                gathers[g].append(go(remote(here, here, acts_send.at[g, n], acts_recv.at[g, n], along_y[j])))

    def acts_cross(g, i, at):
        here = tokens(g, at, 0, HALF)
        gather_crosses[g].append(
            go(remote(here, here, acts_cross_send.at[g, i], acts_cross_recv.at[g, i], partner))
        )

    def acts_forward(g):
        for j in range(2):
            gathers[g][j].wait_recv()
            here, n = tokens(g, ring(y, (-1, 1)[j]), j * QUARTER, QUARTER), 4 + j
            gathers[g].append(go(remote(here, here, acts_send.at[g, n], acts_recv.at[g, n], along_y[j])))
        for j in range(2):
            gathers[g][2 + j].wait_recv()
            acts_cross(g, j, ring(y, (-1, 1)[j]))

    def acts_last(g):
        for copy in gathers[g][4:]:
            copy.wait_recv()
        acts_cross(g, 2, ring(y, 2))

    def acts_ready(g):
        for copy in gather_crosses[g]:
            copy.wait_recv()

    pair.wait_recv()
    acts_first(0)
    acts_first(1)

    count = 2 * GROUPS
    owner = [owners[k] for k in range(count)]
    zero, one = jnp.int32(0), jnp.int32(1)
    slot = []
    for k in range(count):
        slot.append(sum([jnp.where(owner[k2] == owner[k], one, zero) for k2 in range(k)], zero))
        slot_table[k] = jnp.minimum(slot[k], CAP - 1)

    load_grads.wait()
    for xd in range(SIDE):
        for start in range(0, BLK, QUARTER):
            turned[xd, start : start + QUARTER, :] = grads[:, xd * BLK + start : xd * BLK + start + QUARTER].T
    acts_forward(0)
    for copy in load_roots:
        copy.wait()
    acts_last(0)
    roots_swap = go(remote(roots, pair_roots, roots_swap_send.at[0], roots_swap_recv.at[0], partner))

    stages1, stages2, outs, crosses = {}, {}, {}, {}

    def products(r):
        p, v, b = r // PER_HALF, r % PER_HALF, r % SLOTS
        if r < 2:
            acts_ready(r)
        if r == PER_HALF:
            acts_ready(2)
        right = jnp.concatenate([acts[p, v, zd] for zd in range(SIDE)], axis=1)
        for u in range(2):
            if r >= SLOTS:
                stages1[r - SLOTS, u].finish()

            def step(xd, carry, u=u):
                left = turned[xd, u * HALF : (u + 1) * HALF]
                value = jnp.dot(left, right, preferred_element_type=F32).astype(BF16)
                for half in range(2):
                    rows = value[half * QUARTER : (half + 1) * QUARTER]
                    if u == 0:
                        parts[b, 0, xd, half] = rows
                    else:
                        lanes = pl.ds(pl.multiple_of(xd * COLS, COLS), COLS)
                        for zd in range(SIDE):
                            parts[b, 1, zd, half, :, lanes] = rows[:, zd * COLS : (zd + 1) * COLS]
                return carry

            lax.fori_loop(0, SIDE, step, 0)
            me, (right_to, left_to) = ((x, along_x), (z, along_z))[u]
            stage = RingSum(
                parts.at[b, u], me, right_to, left_to, far1.at[b, u], near1.at[b, u], send1.at[b, u], recv1.at[b, u]
            )
            stage.first()
            stages1[r, u] = stage

    def merge1(r):
        for u in range(2):
            stages1[r, u].merge()

    def between(r):
        b = r % SLOTS
        for u in range(2):
            if r >= SLOTS:
                stages2[r - SLOTS, u].finish()
            total = stages1[r, u].total()
            for half in range(2):
                for d in range(SIDE):
                    sums[b, u, d, half] = total[half][:, d * COLS : (d + 1) * COLS]
            me, (right_to, left_to) = ((z, along_z), (x, along_x))[u]
            stage = RingSum(
                sums.at[b, u], me, right_to, left_to, far2.at[b, u], near2.at[b, u], send2.at[b, u], recv2.at[b, u]
            )
            stage.first()
            stages2[r, u] = stage

    def merge2(r):
        for u in range(2):
            stages2[r, u].merge()

    def strip(r, at, half):
        return blocks[r // PER_HALF].at[core, at, r % PER_HALF, pl.ds(half * HALF, HALF)]

    def spread(r):
        for u in range(2):
            total = stages2[r, u].total()
            for half in range(2):
                start = u * HALF + half * QUARTER
                blocks[r // PER_HALF][core, y, r % PER_HALF, start : start + QUARTER] = total[half]
        outs[r] = []
        for i in range(2):
            for j in range(2):
                here = strip(r, y, i ^ j)
                outs[r].append(remote(here, here, out_send.at[r], out_recv.at[r, 2 * i + j], along_y[j]))
                outs[r][-1].start()

    def pass_on(r):
        for j in range(2):
            outs[r][j].wait_recv()
            here = strip(r, ring(y, (-1, 1)[j]), j)
            outs[r].append(remote(here, here, out_send.at[r], out_recv.at[r, 4 + j], along_y[j]))
            outs[r][-1].start()

    def pass_last(r):
        for copy in outs[r][2:]:
            copy.wait_recv()
        here = blocks[r // PER_HALF].at[core, :, r % PER_HALF]
        crosses[r] = go(remote(here, here, cross_send.at[r], cross_recv.at[r], partner))

    def spread_finish(r):
        sent = blocks[r // PER_HALF].at[core, pl.ds(0, SIDE - 1), r % PER_HALF]
        remote(sent, sent, out_send.at[r], out_recv.at[r, 0], partner).wait_send()

    def whole(p, c, at):
        return jnp.concatenate([blocks[p][c, at, v] for v in range(PER_HALF)], axis=1)

    def hold(p):
        shaped = jnp.dot(holder_roots[p, 0], whole(p, core, y), preferred_element_type=F32).astype(BF16)
        product = jnp.dot(shaped, holder_roots[p, 1], preferred_element_type=F32)
        scaling = lax.rsqrt(jnp.mean(product * product) + EPSILON)
        out_ref[p] = (product * scaling).astype(BF16)

    routed = [
        [
            Routed(
                p, owners, slot_table, y, core, along_y, roots.at[n], pair_roots.at[n],
                roots_packed.at[n], roots_far.at[p, n], roots_near.at[p, n], roots_send.at[p, n], roots_recv.at[p, n],
            )
            for n in range(2)
        ]
        for p in range(2)
    ]
    (left0, right0), (left1, right1) = routed

    def collect(s):
        def pick(value):
            return sum([jnp.where((owner[k] == group) & (slot[k] == s), value(k), zero) for k in range(count)], zero)

        odd, used = pick(lambda k: jnp.int32(k % 2)), pick(lambda k: one)
        c, at = pick(lambda k: jnp.int32(k // 2 % 2)), pick(lambda k: jnp.int32(k // 4))
        block = jnp.where(odd > 0, whole(1, c, at), whole(0, c, at))
        owned[s] = jnp.where(used > 0, block, jnp.zeros_like(block))
        copy = pltpu.make_async_copy(owned.at[s], owned_ref.at[s], owned_sem.at[s])
        copy.start()
        return copy

    def at_lag(part, lag):
        if 0 <= step - lag < ROUNDS:
            part(step - lag)

    for step in range(ROUNDS + 4):
        at_lag(products, 0)
        at_lag(spread, 2)
        at_lag(pass_last, 4)
        at_lag(between, 1)
        at_lag(merge1, 0)
        at_lag(merge2, 1)
        at_lag(pass_on, 3)
        if step == 0:
            acts_forward(1)
            roots_swap.wait_recv()
            left1.send(0)
            acts_last(1)
        if step == 1:
            acts_first(2)
            left1.send(1)
        if step == 2:
            acts_forward(2)
            left1.merge()
        if step == 3:
            acts_last(2)
            right1.send(0)
        if step == 4:
            right1.send(1)
            left1.finish()
            left0.send(0)
        if step == 5:
            right1.merge()
        if step == 6:
            left0.send(1)
            right1.finish()
            right0.send(0)
        if step == 7:
            left0.merge()
            right0.send(1)
            left1.last(holder_roots.at[1, 0])
            right1.last(holder_roots.at[1, 1])
        if step == 8:
            right0.merge()
        if step == 9:
            hold(1)
        if step == 10:
            left0.last(holder_roots.at[0, 0])
            right0.last(holder_roots.at[0, 1])
            hold(0)
    for r in range(ROUNDS):
        crosses[r].wait_recv()
    kept = [collect(s) for s in range(CAP)]

    for copy in started:
        copy.wait_send()
    left0.finish()
    right0.finish()
    for r in range(ROUNDS):
        spread_finish(r)
    for r in range(ROUNDS - SLOTS, ROUNDS):
        for u in range(2):
            stages1[r, u].finish()
            stages2[r, u].finish()
    for copy in kept:
        copy.wait()


def gradient_blocks(owners, acts, grads_out, left_root, right_root):
    dma = pltpu.SemaphoreType.DMA
    square, half, wide, small = (BLK, BLK), (HALF, BLK), (QUARTER, BLK), (QUARTER, COLS)
    shapes = [
        (BLK, SIDE * BLK),
        (SIDE,) + square,
        (2, PER_HALF, SIDE, BLK, COLS),
        (SLOTS, 2, SIDE, 2) + wide,
        (SLOTS, 2, 2) + wide,
        (SLOTS, 2, 2, 2) + wide,
        (SLOTS, 2, SIDE, 2) + small,
        (SLOTS, 2, 2) + small,
        (SLOTS, 2, 2, 2) + small,
        (2, SIDE, PER_HALF, BLK, COLS),
        (2, SIDE, PER_HALF, BLK, COLS),
        (2, CAP) + square,
        (2, CAP) + square,
        (2, 3, 2) + half,
        (2, 2, 2) + half,
        (2, 2, 2, 2) + half,
        (2, 2) + square,
        (CAP,) + square,
    ]
    semaphores = [
        (PER_HALF + 3,), (1,), (1,), (3, 6), (3, 6), (3, 3), (3, 3),
        (SLOTS, 2), (SLOTS, 2, 3), (SLOTS, 2), (SLOTS, 2, 3),
        (ROUNDS,), (ROUNDS, 6), (ROUNDS,), (ROUNDS,),
        (1,), (1,), (2, 2), (2, 2, 3), (CAP,),
    ]
    return pl.pallas_call(
        gradient_kernel,
        out_shape=(
            jax.ShapeDtypeStruct((CAP, BLK, BLK), BF16),
            jax.ShapeDtypeStruct((2, BLK, BLK), BF16),
        ),
        in_specs=[pl.BlockSpec(memory_space=pltpu.SMEM)] + [pl.BlockSpec(memory_space=pl.ANY)] * 4,
        out_specs=(pl.BlockSpec(memory_space=pl.ANY), pl.BlockSpec(memory_space=pltpu.VMEM)),
        scratch_shapes=[pltpu.VMEM(shape, BF16) for shape in shapes]
        + [pltpu.SMEM((2 * GROUPS,), jnp.int32)]
        + [dma(shape) for shape in semaphores],
        compiler_params=pltpu.CompilerParams(
            collective_id=0, has_side_effects=True, vmem_limit_bytes=62 << 20
        ),
        cost_estimate=pl.CostEstimate(flops=12 << 30, bytes_accessed=10 << 20, transcendentals=0),
        name="gradient_blocks",
    )(owners, acts, grads_out, left_root, right_root)


def grams_kernel(block_ref, ls_ref, rs_ref, ln_ref, rn_ref):
    block = block_ref[0]
    rows = pl.ds(pl.multiple_of(pl.program_id(1) * TILE, TILE), TILE)
    left = lax.dot_general(block_ref[0, rows], block, (((1,), (1,)), ((), ())), preferred_element_type=F32)
    ln_ref[0, 0, 0] = STAT_DECAY * ls_ref[0, 0, 0] + (1.0 - STAT_DECAY) * left
    right = lax.dot_general(block_ref[0, :, rows], block, (((0,), (0,)), ((), ())), preferred_element_type=F32)
    rn_ref[0, 0, 0] = STAT_DECAY * rs_ref[0, 0, 0] + (1.0 - STAT_DECAY) * right


def grams(owned, left_stats, right_stats):
    part = pl.BlockSpec((1, 1, 1, TILE, BLK), lambda s, i: (0, 0, s, i, 0))
    return pl.pallas_call(
        grams_kernel,
        grid=(CAP, BLK // TILE),
        in_specs=[pl.BlockSpec((1, BLK, BLK), lambda s, i: (s, 0, 0)), part, part],
        out_specs=(part, part),
        out_shape=(
            jax.ShapeDtypeStruct(left_stats.shape, F32),
            jax.ShapeDtypeStruct(right_stats.shape, F32),
        ),
        compiler_params=pltpu.CompilerParams(vmem_limit_bytes=62 << 20),
        name="grams",
    )(owned, left_stats, right_stats)


def body(acts, grads_out, owners, left_stats, right_stats, left_root, right_root):
    owned, update = gradient_blocks(owners.reshape(-1), acts, grads_out, left_root, right_root)
    left_new, right_new = grams(owned, left_stats, right_stats)
    return (left_new, right_new, update)


def solution(mesh):
    placed = (
        P("dp", "group"),
        P("dp", "group"),
        P("dp", None, None),
        P("dp", "group", None, None, None),
        P("dp", "group", None, None, None),
        P("dp", "group", None, None, None),
        P("dp", "group", None, None, None),
    )
    return jax.shard_map(
        body,
        mesh=mesh,
        in_specs=placed,
        out_specs=(
            P("dp", "group", None, None, None),
            P("dp", "group", None, None, None),
            P(("group", "dp"), None, None),
        ),
        check_vma=False,
    )
```

time: 152 us -> 169 us (1.11)
  Pallas kernels: 150 us -> 167 us
    pallas_call x1, Pallas kernels: 143 us -> 159 us  [gradient_blocks(): pl.pallas_call(gradient_kernel, out_shape=(jax.ShapeDtypeStruct((CAP, BLK...]
where the time goes in v5:
time: 169 us; the launch traced here: 168 us
  Pallas kernels  167 us (99%)
    pallas_call x1, Pallas kernels, gradient_blocks(): pl.pallas_call(gradient_kernel, out_shape=(jax.ShapeDtypeStruct((CAP, BLK...  159 us
    pallas_call x1, Pallas kernels, grams(): pl.pallas_call(grams_kernel, grid=(CAP, BLK // TILE), in_specs=[pl.BlockS...  7.34 us

profile of v5, /device:TPU:1, one launch (start us, length us, event | category | flops | bytes accessed | tf_op | source)
XLA Modules:
  0.0 168.4 jit_solution(528675238234002530)
XLA Ops:
  0.6 159.5 %gradient_blocks.1 = (bf16[3,512,512]{2,1,0:T(8,128)(2,1)}, bf16[2,512,512]{2,1,0:T(8,128)(2,1)}) custom-call(s32[16]{0:T(128)} %bitcast.1, bf16[512,512]{1,0:T(8,128)(2,1)} %acts_ref.1, bf16[512,2048]{1,0:T(8,128)(2,1)} %grads_ref.1, bf16[1,1,3,512,512]{4,3,2,1,0:T(8,128)(2,1)} %lr_ref.1, bf16[1,1,3,512,512]{4,3,2,1,0:T(8,128)(2,1)} %rr_ref.1), custom_call_target="tpu_custom_call" | custom-call | flops 12884901888 | bytes 10485760 | tf_op jit(solution)/shard_map/gradient_blocks/pallas_call | solution.py:465
  160.1 0.0 copy-start
  160.1 7.3 %grams.1 = (f32[1,1,3,512,512]{4,3,2,1,0:T(8,128)}, f32[1,1,3,512,512]{4,3,2,1,0:T(8,128)}) custom-call(bf16[3,512,512]{2,1,0:T(8,128)(2,1)} %get-tuple-element.7.block_ref, f32[1,1,3,512,512]{4,3,2,1,0:T(8,128)} %ls_ref.1, f32[1,1,3,512,512]{4,3,2,1,0:T(8,128)} %rs_ref.1), custom_call_target="tpu_custom_call" | custom-call | tf_op jit(solution)/shard_map/grams/pallas_call | solution.py:495
  167.4 0.0 copy-done
  167.4 1.0 copy.11
Async XLA Ops:
  160.1 7.3 %copy-start = (bf16[2,512,512]{2,1,0:T(8,128)(2,1)S(1)}, bf16[2,512,512]{2,1,0:T(8,128)(2,1)}, u32[]{:S(2)}) copy-start(bf16[2,512,512]{2,1,0:T(8,128)(2,1)} %get-tuple-element.16) | copy-start | bytes 3145732

commit v6 on v5

--- a/solution.py
+++ b/solution.py
@@ -16,11 +16,11 @@
 GROUPS = 8
 CAP = 3
 QUARTER = HALF // 2
-TILE = BLK
 COLS = 128
 PER_HALF = BLK // COLS
 ROUNDS = 2 * PER_HALF
 SLOTS = 3
+LAST_LAG = 3
 F32 = jnp.float32
 BF16 = jnp.bfloat16
 
@@ -145,11 +145,13 @@
 def gradient_kernel(
     owners, acts_ref, grads_ref, lr_ref, rr_ref,
     owned_ref, out_ref,
-    grads, turned, acts, parts, far1, near1, sums, far2, near2, blocks0, blocks1,
-    roots, pair_roots, roots_packed, roots_far, roots_near, holder_roots, owned, slot_table,
+    grads, turned, acts, parts, far1, near1, sums, far2, near2,
+    roots, pair_roots, roots_packed, roots_far, roots_near, holder_roots,
+    result, held, packed, back_far, back_near, owned, shaped, slot_table, rank_table, mine_table,
     local_sem, pair_send, pair_recv, acts_send, acts_recv, acts_cross_send, acts_cross_recv,
     send1, recv1, send2, recv2, out_send, out_recv, cross_send, cross_recv,
-    roots_swap_send, roots_swap_recv, roots_send, roots_recv, owned_sem,
+    roots_swap_send, roots_swap_recv, roots_send, roots_recv, swap_send, swap_recv, back_send, back_recv, owned_sem,
+    *blocks,
 ):
     x, y, z, core = place()
     group = y * 2 + core
@@ -157,7 +159,6 @@
     along_y = [device(x, ring(y, s), z, core) for s in (1, -1)]
     along_x = [device(ring(x, s), y, z, core) for s in (1, -1)]
     along_z = [device(x, y, ring(z, s), core) for s in (1, -1)]
-    blocks = (blocks0, blocks1)
     started = []
 
     def go(copy):
@@ -227,10 +228,28 @@
     count = 2 * GROUPS
     owner = [owners[k] for k in range(count)]
     zero, one = jnp.int32(0), jnp.int32(1)
-    slot = []
+    slot, rank = [], []
     for k in range(count):
-        slot.append(sum([jnp.where(owner[k2] == owner[k], one, zero) for k2 in range(k)], zero))
+        same = [jnp.where(owner[k2] == owner[k], one, zero) for k2 in range(k)]
+        slot.append(sum(same, zero))
+        rank.append(sum(same[0::2], zero))
         slot_table[k] = jnp.minimum(slot[k], CAP - 1)
+        rank_table[k] = jnp.minimum(rank[k], CAP - 1)
+    is_mine = [owner[k] == group for k in range(count)]
+
+    def pick(positions, test, value):
+        return sum([jnp.where(is_mine[k] & test(k), value(k), zero) for k in positions], zero)
+
+    for j in range(CAP):
+        even, test = range(0, count, 2), lambda k, j=j: rank[k] == j
+        mine_table[3 * j] = pick(even, test, lambda k: jnp.int32(k // 2 % 2))
+        mine_table[3 * j + 1] = pick(even, test, lambda k: jnp.int32(k // 4))
+        mine_table[3 * j + 2] = pick(even, test, lambda k: jnp.minimum(slot[k], CAP - 1))
+        every, test, at = range(count), lambda k, j=j: slot[k] == j, 3 * CAP + 4 * j
+        mine_table[at] = pick(every, test, lambda k: jnp.int32(k % 2))
+        mine_table[at + 1] = pick(every, test, lambda k: one)
+        mine_table[at + 2] = pick(every, test, lambda k: jnp.int32(k // 2 % 2))
+        mine_table[at + 3] = pick(every, test, lambda k: jnp.int32(k // 4))
 
     load_grads.wait()
     for xd in range(SIDE):
@@ -255,20 +274,17 @@
             if r >= SLOTS:
                 stages1[r - SLOTS, u].finish()
 
-            def step(xd, carry, u=u):
-                left = turned[xd, u * HALF : (u + 1) * HALF]
-                value = jnp.dot(left, right, preferred_element_type=F32).astype(BF16)
+            left = turned[:, u * HALF : (u + 1) * HALF].reshape(SIDE * HALF, BLK)
+            value = jnp.dot(left, right, preferred_element_type=F32).astype(BF16)
+            for xd in range(SIDE):
                 for half in range(2):
-                    rows = value[half * QUARTER : (half + 1) * QUARTER]
+                    rows = value[xd * HALF + half * QUARTER : xd * HALF + (half + 1) * QUARTER]
                     if u == 0:
                         parts[b, 0, xd, half] = rows
                     else:
-                        lanes = pl.ds(pl.multiple_of(xd * COLS, COLS), COLS)
                         for zd in range(SIDE):
-                            parts[b, 1, zd, half, :, lanes] = rows[:, zd * COLS : (zd + 1) * COLS]
-                return carry
-
-            lax.fori_loop(0, SIDE, step, 0)
+                            lanes = slice(zd * COLS, (zd + 1) * COLS)
+                            parts[b, 1, zd, half, :, xd * COLS : (xd + 1) * COLS] = rows[:, lanes]
             me, (right_to, left_to) = ((x, along_x), (z, along_z))[u]
             stage = RingSum(
                 parts.at[b, u], me, right_to, left_to, far1.at[b, u], near1.at[b, u], send1.at[b, u], recv1.at[b, u]
@@ -301,14 +317,14 @@
             stages2[r, u].merge()
 
     def strip(r, at, half):
-        return blocks[r // PER_HALF].at[core, at, r % PER_HALF, pl.ds(half * HALF, HALF)]
+        return blocks[r].at[core, at, pl.ds(half * HALF, HALF)]
 
     def spread(r):
         for u in range(2):
             total = stages2[r, u].total()
             for half in range(2):
                 start = u * HALF + half * QUARTER
-                blocks[r // PER_HALF][core, y, r % PER_HALF, start : start + QUARTER] = total[half]
+                blocks[r][core, y, start : start + QUARTER] = total[half]
         outs[r] = []
         for i in range(2):
             for j in range(2):
@@ -326,58 +342,83 @@
     def pass_last(r):
         for copy in outs[r][2:]:
             copy.wait_recv()
-        here = blocks[r // PER_HALF].at[core, :, r % PER_HALF]
+        here = blocks[r].at[core]
         crosses[r] = go(remote(here, here, cross_send.at[r], cross_recv.at[r], partner))
 
     def spread_finish(r):
-        sent = blocks[r // PER_HALF].at[core, pl.ds(0, SIDE - 1), r % PER_HALF]
+        sent = blocks[r].at[core, pl.ds(0, SIDE - 1)]
         remote(sent, sent, out_send.at[r], out_recv.at[r, 0], partner).wait_send()
 
-    def whole(p, c, at):
-        return jnp.concatenate([blocks[p][c, at, v] for v in range(PER_HALF)], axis=1)
-
-    def hold(p):
-        shaped = jnp.dot(holder_roots[p, 0], whole(p, core, y), preferred_element_type=F32).astype(BF16)
-        product = jnp.dot(shaped, holder_roots[p, 1], preferred_element_type=F32)
+    def condition(shaped_block, right_root):
+        product = jnp.dot(shaped_block, right_root, preferred_element_type=F32)
         scaling = lax.rsqrt(jnp.mean(product * product) + EPSILON)
-        out_ref[p] = (product * scaling).astype(BF16)
-
-    routed = [
-        [
-            Routed(
-                p, owners, slot_table, y, core, along_y, roots.at[n], pair_roots.at[n],
-                roots_packed.at[n], roots_far.at[p, n], roots_near.at[p, n], roots_send.at[p, n], roots_recv.at[p, n],
-            )
-            for n in range(2)
-        ]
-        for p in range(2)
+        return (product * scaling).astype(BF16)
+
+    swaps = []
+
+    def shape_part(v):
+        for j in range(CAP):
+            c, to, at = [mine_table[3 * j + i] for i in range(3)]
+            pair_of = jnp.concatenate([blocks[v][c, to], blocks[v + 1][c, to]], axis=1)
+            value = jnp.dot(roots[0, at], pair_of, preferred_element_type=F32)
+            shaped[j, :, v * COLS : (v + 2) * COLS] = value.astype(BF16)
+
+    def precondition():
+        for j in range(CAP):
+            result[j] = condition(shaped[j], roots[1, mine_table[3 * j + 2]])
+            swaps.append(go(remote(result.at[j], held.at[j], swap_send.at[j], swap_recv.at[j], partner)))
+
+    back = Routed(
+        0, owners, rank_table, y, core, along_y, result, held, packed, back_far, back_near, back_send.at[0], back_recv
+    )
+    left1, right1 = [
+        Routed(
+            1, owners, slot_table, y, core, along_y, roots.at[n], pair_roots.at[n],
+            roots_packed.at[n], roots_far.at[n], roots_near.at[n], roots_send.at[n], roots_recv.at[n],
+        )
+        for n in range(2)
     ]
-    (left0, right0), (left1, right1) = routed
-
-    def collect(s):
-        def pick(value):
-            return sum([jnp.where((owner[k] == group) & (slot[k] == s), value(k), zero) for k in range(count)], zero)
-
-        odd, used = pick(lambda k: jnp.int32(k % 2)), pick(lambda k: one)
-        c, at = pick(lambda k: jnp.int32(k // 2 % 2)), pick(lambda k: jnp.int32(k // 4))
-        block = jnp.where(odd > 0, whole(1, c, at), whole(0, c, at))
-        owned[s] = jnp.where(used > 0, block, jnp.zeros_like(block))
-        copy = pltpu.make_async_copy(owned.at[s], owned_ref.at[s], owned_sem.at[s])
-        copy.start()
-        return copy
+
+    def collect(r):
+        p, cols = r // PER_HALF, slice(r % PER_HALF * COLS, (r % PER_HALF + 1) * COLS)
+        for s in range(CAP):
+            odd, used, c, at = [mine_table[3 * CAP + 4 * s + i] for i in range(4)]
+            value = blocks[r][c, at]
+            if p == 0:
+                owned[s, :, cols] = jnp.where((used > 0) & (odd == 0), value, jnp.zeros_like(value))
+            else:
+                owned[s, :, cols] = jnp.where(odd > 0, value, owned[s, :, cols])
 
     def at_lag(part, lag):
         if 0 <= step - lag < ROUNDS:
             part(step - lag)
 
+    half_done = PER_HALF - 1 + LAST_LAG
     for step in range(ROUNDS + 4):
         at_lag(products, 0)
         at_lag(spread, 2)
-        at_lag(pass_last, 4)
+        if step == half_done and LAST_LAG < 4:
+            pass_last(PER_HALF - 2)
+            pass_last(PER_HALF - 1)
+        elif step not in (half_done, half_done + 1) or LAST_LAG == 4:
+            at_lag(pass_last, 4)
+        if step == half_done:
+            crosses[2].wait_recv()
+            crosses[3].wait_recv()
+            shape_part(2)
+            precondition()
         at_lag(between, 1)
         at_lag(merge1, 0)
         at_lag(merge2, 1)
-        at_lag(pass_on, 3)
+        if step == half_done - 1:
+            crosses[0].wait_recv()
+            crosses[1].wait_recv()
+            shape_part(0)
+        if LAST_LAG < 4 and step == half_done - 1:
+            pass_on(PER_HALF - 2)
+            pass_on(PER_HALF - 1)
+        elif LAST_LAG == 4 or step != half_done:
+            at_lag(pass_on, 3)
         if step == 0:
             acts_forward(1)
             roots_swap.wait_recv()
@@ -394,35 +435,40 @@
             right1.send(0)
         if step == 4:
             right1.send(1)
-            left1.finish()
-            left0.send(0)
         if step == 5:
             right1.merge()
-        if step == 6:
-            left0.send(1)
-            right1.finish()
-            right0.send(0)
-        if step == 7:
-            left0.merge()
-            right0.send(1)
-            left1.last(holder_roots.at[1, 0])
-            right1.last(holder_roots.at[1, 1])
+        if step == half_done:
+            for copy in swaps:
+                copy.wait_recv()
+            back.send(0)
+            back.send(1)
+        if step == half_done + 1:
+            back.merge()
         if step == 8:
-            right0.merge()
+            left1.last(holder_roots.at[0])
+            right1.last(holder_roots.at[1])
+            for r in range(PER_HALF):
+                collect(r)
         if step == 9:
-            hold(1)
+            block = jnp.concatenate([blocks[PER_HALF + v][core, y] for v in range(PER_HALF)], axis=1)
+            block = jnp.dot(holder_roots[0], block, preferred_element_type=F32).astype(BF16)
+            out_ref[1] = condition(block, holder_roots[1])
         if step == 10:
-            left0.last(holder_roots.at[0, 0])
-            right0.last(holder_roots.at[0, 1])
-            hold(0)
-    for r in range(ROUNDS):
-        crosses[r].wait_recv()
-    kept = [collect(s) for s in range(CAP)]
+            back.last(out_ref.at[0])
+        if step >= 9:
+            crosses[step - 5].wait_recv()
+            collect(step - 5)
+    crosses[ROUNDS - 1].wait_recv()
+    collect(ROUNDS - 1)
+    kept = []
+    for s in range(CAP):
+        kept.append(pltpu.make_async_copy(owned.at[s], owned_ref.at[s], owned_sem.at[s]))
+        kept[s].start()
 
     for copy in started:
         copy.wait_send()
-    left0.finish()
-    right0.finish()
+    for part in (left1, right1, back):
+        part.finish()
     for r in range(ROUNDS):
         spread_finish(r)
     for r in range(ROUNDS - SLOTS, ROUNDS):
@@ -446,21 +492,25 @@
         (SLOTS, 2, SIDE, 2) + small,
         (SLOTS, 2, 2) + small,
         (SLOTS, 2, 2, 2) + small,
-        (2, SIDE, PER_HALF, BLK, COLS),
-        (2, SIDE, PER_HALF, BLK, COLS),
         (2, CAP) + square,
         (2, CAP) + square,
         (2, 3, 2) + half,
+        (2, 2) + half,
         (2, 2, 2) + half,
-        (2, 2, 2, 2) + half,
-        (2, 2) + square,
+        (2,) + square,
+        (CAP,) + square,
+        (CAP,) + square,
+        (3, 2) + half,
+        (2,) + half,
+        (2, 2) + half,
+        (CAP,) + square,
         (CAP,) + square,
     ]
     semaphores = [
         (PER_HALF + 3,), (1,), (1,), (3, 6), (3, 6), (3, 3), (3, 3),
         (SLOTS, 2), (SLOTS, 2, 3), (SLOTS, 2), (SLOTS, 2, 3),
         (ROUNDS,), (ROUNDS, 6), (ROUNDS,), (ROUNDS,),
-        (1,), (1,), (2, 2), (2, 2, 3), (CAP,),
+        (1,), (1,), (2,), (2, 3), (CAP,), (CAP,), (1,), (3,), (CAP,),
     ]
     return pl.pallas_call(
         gradient_kernel,
@@ -471,8 +521,10 @@
         in_specs=[pl.BlockSpec(memory_space=pltpu.SMEM)] + [pl.BlockSpec(memory_space=pl.ANY)] * 4,
         out_specs=(pl.BlockSpec(memory_space=pl.ANY), pl.BlockSpec(memory_space=pltpu.VMEM)),
         scratch_shapes=[pltpu.VMEM(shape, BF16) for shape in shapes]
-        + [pltpu.SMEM((2 * GROUPS,), jnp.int32)]
-        + [dma(shape) for shape in semaphores],
+        + [pltpu.SMEM((2 * GROUPS,), jnp.int32)] * 2
+        + [pltpu.SMEM((7 * CAP,), jnp.int32)]
+        + [dma(shape) for shape in semaphores]
+        + [pltpu.VMEM((2, SIDE, BLK, COLS), BF16)] * ROUNDS,
         compiler_params=pltpu.CompilerParams(
             collective_id=0, has_side_effects=True, vmem_limit_bytes=62 << 20
         ),
@@ -481,35 +533,67 @@
     )(owners, acts, grads_out, left_root, right_root)
 
 
-def grams_kernel(block_ref, ls_ref, rs_ref, ln_ref, rn_ref):
-    block = block_ref[0]
-    rows = pl.ds(pl.multiple_of(pl.program_id(1) * TILE, TILE), TILE)
-    left = lax.dot_general(block_ref[0, rows], block, (((1,), (1,)), ((), ())), preferred_element_type=F32)
-    ln_ref[0, 0, 0] = STAT_DECAY * ls_ref[0, 0, 0] + (1.0 - STAT_DECAY) * left
-    right = lax.dot_general(block_ref[0, :, rows], block, (((0,), (0,)), ((), ())), preferred_element_type=F32)
-    rn_ref[0, 0, 0] = STAT_DECAY * rs_ref[0, 0, 0] + (1.0 - STAT_DECAY) * right
-
-
-def grams(owned, left_stats, right_stats):
-    part = pl.BlockSpec((1, 1, 1, TILE, BLK), lambda s, i: (0, 0, s, i, 0))
+def grams_kernel(
+    owned_ref, ls_ref, rs_ref, held_ref, ln_ref, rn_ref, out_ref, owned, left_stats, right_stats, held, load_sem, store_sem, held_sem
+):
+    loads = [
+        [
+            pltpu.make_async_copy(ls_ref.at[0, 0, s], left_stats.at[s], load_sem.at[s, 0]),
+            pltpu.make_async_copy(rs_ref.at[0, 0, s], right_stats.at[s], load_sem.at[s, 1]),
+            pltpu.make_async_copy(owned_ref.at[s], owned.at[s], load_sem.at[s, 2]),
+        ]
+        for s in range(CAP)
+    ]
+    for copies in loads:
+        for copy in copies:
+            copy.start()
+    load_held = pltpu.make_async_copy(held_ref, held, held_sem.at[0])
+    load_held.start()
+    stores = [pltpu.make_async_copy(held, out_ref, held_sem.at[1])]
+    for s in range(CAP):
+        for copy in loads[s]:
+            copy.wait()
+        block = owned[s]
+        sides = ((left_stats, ln_ref, 1), (right_stats, rn_ref, 0))
+        for i, (stats, new_ref, dim) in enumerate(sides):
+            gram = lax.dot_general(block, block, (((dim,), (dim,)), ((), ())), preferred_element_type=F32)
+            stats[s] = STAT_DECAY * stats[s] + (1.0 - STAT_DECAY) * gram
+            store = pltpu.make_async_copy(stats.at[s], new_ref.at[0, 0, s], store_sem.at[s, i])
+            store.start()
+            stores.append(store)
+        if s == CAP - 2:
+            load_held.wait()
+            stores[0].start()
+    for store in stores:
+        store.wait()
+
+
+def grams(owned, left_stats, right_stats, update):
+    dma = pltpu.SemaphoreType.DMA
     return pl.pallas_call(
         grams_kernel,
-        grid=(CAP, BLK // TILE),
-        in_specs=[pl.BlockSpec((1, BLK, BLK), lambda s, i: (s, 0, 0)), part, part],
-        out_specs=(part, part),
+        in_specs=[pl.BlockSpec(memory_space=pl.ANY)] * 4,
+        out_specs=[pl.BlockSpec(memory_space=pl.ANY)] * 3,
         out_shape=(
             jax.ShapeDtypeStruct(left_stats.shape, F32),
             jax.ShapeDtypeStruct(right_stats.shape, F32),
+            jax.ShapeDtypeStruct(update.shape, BF16),
         ),
+        scratch_shapes=[
+            pltpu.VMEM((CAP, BLK, BLK), BF16),
+            pltpu.VMEM((CAP, BLK, BLK), F32),
+            pltpu.VMEM((CAP, BLK, BLK), F32),
+            pltpu.VMEM(update.shape, BF16),
+            dma((CAP, 3)), dma((CAP, 2)), dma((2,)),
+        ],
         compiler_params=pltpu.CompilerParams(vmem_limit_bytes=62 << 20),
         name="grams",
-    )(owned, left_stats, right_stats)
+    )(owned, left_stats, right_stats, update)
 
 
 def body(acts, grads_out, owners, left_stats, right_stats, left_root, right_root):
     owned, update = gradient_blocks(owners.reshape(-1), acts, grads_out, left_root, right_root)
-    left_new, right_new = grams(owned, left_stats, right_stats)
-    return (left_new, right_new, update)
+    return grams(owned, left_stats, right_stats, update)
 
 
 def solution(mesh):

time: 169 us -> 151 us (0.89)
  Pallas kernels: 167 us -> 150 us
    pallas_call x1, Pallas kernels: 159 us -> 143 us  [gradient_blocks(): pl.pallas_call(gradient_kernel, out_shape=(jax.ShapeDtypeStruct((CAP, BLK...]
where the time goes in v6:
time: 151 us
  Pallas kernels  150 us (99%)
    pallas_call x1, Pallas kernels, gradient_blocks(): pl.pallas_call(gradient_kernel, out_shape=(jax.ShapeDtypeStruct((CAP, BLK...  143 us
    pallas_call x1, Pallas kernels, grams(): pl.pallas_call(grams_kernel, in_specs=[pl.BlockSpec(memory_space=pl.ANY)]...  6.6 us

profile of v6, /device:TPU:1, one launch (start us, length us, event | category | flops | bytes accessed | tf_op | source)
XLA Modules:
  0.0 150.9 jit_solution(12451369629426728289)
XLA Ops:
  0.6 143.5 %gradient_blocks.1 = (bf16[3,512,512]{2,1,0:T(8,128)(2,1)}, bf16[2,512,512]{2,1,0:T(8,128)(2,1)}) custom-call(s32[16]{0:T(128)} %bitcast.1, bf16[512,512]{1,0:T(8,128)(2,1)} %acts_ref.1, bf16[512,2048]{1,0:T(8,128)(2,1)} %grads_ref.1, bf16[1,1,3,512,512]{4,3,2,1,0:T(8,128)(2,1)} %lr_ref.1, bf16[1,1,3,512,512]{4,3,2,1,0:T(8,128)(2,1)} %rr_ref.1), custom_call_target="tpu_custom_call" | custom-call | flops 12884901888 | bytes 10485760 | tf_op jit(solution)/shard_map/gradient_blocks/pallas_call | solution.py:515
  144.1 6.6 %grams.1 = (f32[1,1,3,512,512]{4,3,2,1,0:T(8,128)}, f32[1,1,3,512,512]{4,3,2,1,0:T(8,128)}, bf16[2,512,512]{2,1,0:T(8,128)(2,1)}) custom-call(bf16[3,512,512]{2,1,0:T(8,128)(2,1)} %get-tuple-element.5.owned_ref, f32[1,1,3,512,512]{4,3,2,1,0:T(8,128)} %ls_ref.1, f32[1,1,3,512,512]{4,3,2,1,0:T(8,128)} %rs_ref.1, bf16[2,512,512]{2,1,0:T(8,128)(2,1)} %get-tuple-element.6.held_ref), custom_call_target="tpu_custom_call" | custom-call | tf_op jit(solution)/shard_map/grams/pallas_call | solution.py:573

commit v7 on v4

--- a/solution.py
+++ b/solution.py
@@ -16,13 +16,12 @@
 GROUPS = 8
 CAP = 3
 QUARTER = HALF // 2
-TILE = BLK
 SIZES = (64, 64, 64, 64, 64, 64, 64, 64)
 ROUNDS = len(SIZES)
 PER_HALF = ROUNDS // 2
 LARGEST = max(SIZES)
 STARTS = [2 * sum(SIZES[r - r % PER_HALF : r]) for r in range(ROUNDS)]
-SLOTS = 4
+SLOTS = 3
 MERGE1, BETWEEN, MERGE2, SPREAD, PASS_ON, PASS_LAST = 0, 1, 1, 2, 2, 3
 F32 = jnp.float32
 BF16 = jnp.bfloat16
@@ -62,24 +61,23 @@
 
 
 class RingSum:
-    def __init__(self, part, me, right, left, far, near, send, recv):
-        self.part, self.me = part, me
-        to_right = [
-            (part(ring(me, 2)).at[0], far.at[0]),
-            (part(ring(me, 1)).at[1], near.at[0, 1]),
-            (part(ring(me, 1)).at[0], near.at[0, 0]),
+    def __init__(self, parts, me, right, left, far, near, send, recv):
+        self.parts, self.me, self.far, self.near = parts, me, far, near
+
+        def copy(d, half, dst, recv_sem, target):
+            return remote(parts.at[ring(me, d), half], dst, send, recv_sem, target)
+
+        self.copies = [
+            copy(2, 0, far.at[0], recv.at[0], right),
+            copy(2, 1, far.at[1], recv.at[1], left),
+            copy(1, 1, near.at[0, 1], recv.at[2], right),
+            copy(-1, 0, near.at[1, 0], recv.at[2], left),
+            copy(1, 0, near.at[0, 0], recv.at[2], right),
+            copy(-1, 1, near.at[1, 1], recv.at[2], left),
         ]
-        to_left = [
-            (part(ring(me, 2)).at[1], far.at[1]),
-            (part(ring(me, -1)).at[0], near.at[1, 0]),
-            (part(ring(me, -1)).at[1], near.at[1, 1]),
-        ]
-        self.far, self.near = far, near
-        self.copies = []
-        for i in range(3):
-            for j, (target, lists) in enumerate(((right, to_right), (left, to_left))):
-                src, dst = lists[i]
-                self.copies.append(remote(src, dst, send.at[2 * i + j], recv.at[2 * i + j], target))
+        sent = parts.at[pl.ds(0, SIDE - 1)]
+        self.all_sent = remote(sent, sent, send, recv.at[2], right)
+        self.all_near = remote(near, near, send, recv.at[2], right)
 
     def first(self):
         for copy in self.copies[:4]:
@@ -88,19 +86,16 @@
     def merge(self):
         for j, (step, half) in enumerate(((1, 0), (-1, 1))):
             self.copies[j].wait_recv()
-            ref = self.part(ring(self.me, step)).at[half]
-            ref[...] = plus(ref[...], self.far[j])
+            at = ring(self.me, step)
+            self.parts[at, half] = plus(self.parts[at, half], self.far[j])
             self.copies[4 + j].start()
 
     def total(self):
-        for copy in self.copies[2:]:
-            copy.wait_recv()
-        mine = self.part(self.me)
-        return [plus(mine[half], self.near[0, half], self.near[1, half]) for half in range(2)]
+        self.all_near.wait_recv()
+        return [plus(self.parts[self.me, half], self.near[0, half], self.near[1, half]) for half in range(2)]
 
     def finish(self):
-        for copy in self.copies:
-            copy.wait_send()
+        self.all_sent.wait_send()
 
 
 def gradient_kernel(
@@ -231,10 +226,8 @@
 
             lax.fori_loop(0, SIDE, step, 0)
             me, (right, left_to) = ((x, along_x), (z, along_z))[u]
-            rows = pl.ds(0, size)
             stage = RingSum(
-                lambda d, u=u: parts.at[b, u, d, :, :, rows], me, right, left_to,
-                far1.at[b, u, :, :, rows], near1.at[b, u, :, :, :, rows], send1.at[b, u], recv1.at[b, u],
+                parts.at[b, u], me, right, left_to, far1.at[b, u], near1.at[b, u], send1.at[b, u], recv1.at[b, u]
             )
             stage.first()
             stages1[r, u] = stage
@@ -254,10 +247,8 @@
                     for piece in range(2):
                         sums[b, u, half * 2 + o, piece, 0:size] = total[half][o, piece * size : (piece + 1) * size]
             me, (right, left_to) = ((z, along_z), (x, along_x))[u]
-            rows = pl.ds(0, size)
             stage = RingSum(
-                lambda d, u=u: sums.at[b, u, d, :, rows], me, right, left_to,
-                far2.at[b, u, :, rows], near2.at[b, u, :, :, rows], send2.at[b, u], recv2.at[b, u],
+                sums.at[b, u], me, right, left_to, far2.at[b, u], near2.at[b, u], send2.at[b, u], recv2.at[b, u]
             )
             stage.first()
             stages2[r, u] = stage
@@ -492,7 +483,7 @@
     ]
     semaphores = [
         (4,), (1,), (1,), (2, 6), (2, 6), (2, 3), (2, 3),
-        (SLOTS, 2, 6), (SLOTS, 2, 6), (SLOTS, 2, 6), (SLOTS, 2, 6),
+        (SLOTS, 2), (SLOTS, 2, 3), (SLOTS, 2), (SLOTS, 2, 3),
         (ROUNDS, 6), (ROUNDS, 6), (ROUNDS, 4), (ROUNDS, 4),
         (CAP,), (CAP,), (6,), (6,), (1,), (1,), (2, 6), (2, 6), (CAP,),
     ]
@@ -515,35 +506,67 @@
     )(owners, acts, grads_out, left_root, right_root)
 
 
-def grams_kernel(block_ref, ls_ref, rs_ref, ln_ref, rn_ref):
-    block = block_ref[0]
-    rows = pl.ds(pl.multiple_of(pl.program_id(1) * TILE, TILE), TILE)
-    left = lax.dot_general(block_ref[0, rows], block, (((1,), (1,)), ((), ())), preferred_element_type=F32)
-    ln_ref[0, 0, 0] = STAT_DECAY * ls_ref[0, 0, 0] + (1.0 - STAT_DECAY) * left
-    right = lax.dot_general(block_ref[0, :, rows], block, (((0,), (0,)), ((), ())), preferred_element_type=F32)
-    rn_ref[0, 0, 0] = STAT_DECAY * rs_ref[0, 0, 0] + (1.0 - STAT_DECAY) * right
-
-
-def grams(owned, left_stats, right_stats):
-    part = pl.BlockSpec((1, 1, 1, TILE, BLK), lambda s, i: (0, 0, s, i, 0))
+def grams_kernel(
+    owned_ref, ls_ref, rs_ref, held_ref, ln_ref, rn_ref, out_ref, owned, left_stats, right_stats, held, load_sem, store_sem, held_sem
+):
+    loads = [
+        [
+            pltpu.make_async_copy(ls_ref.at[0, 0, s], left_stats.at[s], load_sem.at[s, 0]),
+            pltpu.make_async_copy(rs_ref.at[0, 0, s], right_stats.at[s], load_sem.at[s, 1]),
+            pltpu.make_async_copy(owned_ref.at[s], owned.at[s], load_sem.at[s, 2]),
+        ]
+        for s in range(CAP)
+    ]
+    for copies in loads:
+        for copy in copies:
+            copy.start()
+    load_held = pltpu.make_async_copy(held_ref, held, held_sem.at[0])
+    load_held.start()
+    stores = [pltpu.make_async_copy(held, out_ref, held_sem.at[1])]
+    for s in range(CAP):
+        for copy in loads[s]:
+            copy.wait()
+        block = owned[s]
+        sides = ((left_stats, ln_ref, 1), (right_stats, rn_ref, 0))
+        for i, (stats, new_ref, dim) in enumerate(sides):
+            gram = lax.dot_general(block, block, (((dim,), (dim,)), ((), ())), preferred_element_type=F32)
+            stats[s] = STAT_DECAY * stats[s] + (1.0 - STAT_DECAY) * gram
+            store = pltpu.make_async_copy(stats.at[s], new_ref.at[0, 0, s], store_sem.at[s, i])
+            store.start()
+            stores.append(store)
+        if s == CAP - 2:
+            load_held.wait()
+            stores[0].start()
+    for store in stores:
+        store.wait()
+
+
+def grams(owned, left_stats, right_stats, update):
+    dma = pltpu.SemaphoreType.DMA
     return pl.pallas_call(
         grams_kernel,
-        grid=(CAP, BLK // TILE),
-        in_specs=[pl.BlockSpec((1, BLK, BLK), lambda s, i: (s, 0, 0)), part, part],
-        out_specs=(part, part),
+        in_specs=[pl.BlockSpec(memory_space=pl.ANY)] * 4,
+        out_specs=[pl.BlockSpec(memory_space=pl.ANY)] * 3,
         out_shape=(
             jax.ShapeDtypeStruct(left_stats.shape, F32),
             jax.ShapeDtypeStruct(right_stats.shape, F32),
+            jax.ShapeDtypeStruct(update.shape, BF16),
         ),
+        scratch_shapes=[
+            pltpu.VMEM((CAP, BLK, BLK), BF16),
+            pltpu.VMEM((CAP, BLK, BLK), F32),
+            pltpu.VMEM((CAP, BLK, BLK), F32),
+            pltpu.VMEM(update.shape, BF16),
+            dma((CAP, 3)), dma((CAP, 2)), dma((2,)),
+        ],
         compiler_params=pltpu.CompilerParams(vmem_limit_bytes=62 << 20),
         name="grams",
-    )(owned, left_stats, right_stats)
+    )(owned, left_stats, right_stats, update)
 
 
 def body(acts, grads_out, owners, left_stats, right_stats, left_root, right_root):
     owned, update = gradient_blocks(owners.reshape(-1), acts, grads_out, left_root, right_root)
-    left_new, right_new = grams(owned, left_stats, right_stats)
-    return (left_new, right_new, update)
+    return grams(owned, left_stats, right_stats, update)
 
 
 def solution(mesh):

time: 152 us -> 149 us (0.980)
  Pallas kernels: 150 us -> 148 us
where the time goes in v7:
time: 149 us
  Pallas kernels  148 us (99%)
    pallas_call x1, Pallas kernels, gradient_blocks(): pl.pallas_call(gradient_kernel, out_shape=(jax.ShapeDtypeStruct((CAP, BLK...  142 us
    pallas_call x1, Pallas kernels, grams(): pl.pallas_call(grams_kernel, in_specs=[pl.BlockSpec(memory_space=pl.ANY)]...  6.6 us

profile of v7, /device:TPU:1, one launch (start us, length us, event | category | flops | bytes accessed | tf_op | source)
XLA Modules:
  0.0 149.0 jit_solution(956640085940308797)
XLA Ops:
  0.6 141.6 %gradient_blocks.1 = (bf16[3,512,512]{2,1,0:T(8,128)(2,1)}, bf16[2,512,512]{2,1,0:T(8,128)(2,1)}) custom-call(s32[16]{0:T(128)} %bitcast.1, bf16[512,512]{1,0:T(8,128)(2,1)} %acts_ref.1, bf16[512,2048]{1,0:T(8,128)(2,1)} %grads_ref.1, bf16[1,1,3,512,512]{4,3,2,1,0:T(8,128)(2,1)} %lr_ref.1, bf16[1,1,3,512,512]{4,3,2,1,0:T(8,128)(2,1)} %rr_ref.1), custom_call_target="tpu_custom_call" | custom-call | flops 12884901888 | bytes 10485760 | tf_op jit(solution)/shard_map/gradient_blocks/pallas_call | solution.py:490
  142.2 6.6 %grams.1 = (f32[1,1,3,512,512]{4,3,2,1,0:T(8,128)}, f32[1,1,3,512,512]{4,3,2,1,0:T(8,128)}, bf16[2,512,512]{2,1,0:T(8,128)(2,1)}) custom-call(bf16[3,512,512]{2,1,0:T(8,128)(2,1)} %get-tuple-element.5.owned_ref, f32[1,1,3,512,512]{4,3,2,1,0:T(8,128)} %ls_ref.1, f32[1,1,3,512,512]{4,3,2,1,0:T(8,128)} %rs_ref.1, bf16[2,512,512]{2,1,0:T(8,128)(2,1)} %get-tuple-element.6.held_ref), custom_call_target="tpu_custom_call" | custom-call | tf_op jit(solution)/shard_map/grams/pallas_call | solution.py:546

commit v8 on v7

--- a/solution.py
+++ b/solution.py
@@ -275,14 +275,16 @@
         for i in range(2):
             for j in range(2):
                 here, n = strip(r, group, (i ^ j) * size, size), 2 * i + j
-                outs[r].append(go(remote(here, here, out_send.at[r, n], out_recv.at[r, n], along_y[j])))
+                outs[r].append(remote(here, here, out_send.at[r], out_recv.at[r, n], along_y[j]))
+                outs[r][-1].start()
         cross(r, 0, group)
 
     def pass_on(r):
         for j in range(2):
             outs[r][j].wait_recv()
             here, n = strip(r, 2 * ring(y, (-1, 1)[j]) + core, j * SIZES[r], SIZES[r]), 4 + j
-            outs[r].append(go(remote(here, here, out_send.at[r, n], out_recv.at[r, n], along_y[j])))
+            outs[r].append(remote(here, here, out_send.at[r], out_recv.at[r, n], along_y[j]))
+            outs[r][-1].start()
         for j in range(2):
             outs[r][2 + j].wait_recv()
             cross(r, 1 + j, 2 * ring(y, (-1, 1)[j]) + core)
@@ -445,6 +447,9 @@
 
     for copy in started:
         copy.wait_send()
+    for r in range(ROUNDS):
+        sent = blocks[r // PER_HALF].at[pl.ds(0, SIDE - 1), pl.ds(STARTS[r], 2 * SIZES[r])]
+        remote(sent, sent, out_send.at[r], out_recv.at[r, 0], partner).wait_send()
     for r in range(ROUNDS - SLOTS, ROUNDS):
         for u in range(2):
             stages1[r, u].finish()
@@ -484,7 +489,7 @@
     semaphores = [
         (4,), (1,), (1,), (2, 6), (2, 6), (2, 3), (2, 3),
         (SLOTS, 2), (SLOTS, 2, 3), (SLOTS, 2), (SLOTS, 2, 3),
-        (ROUNDS, 6), (ROUNDS, 6), (ROUNDS, 4), (ROUNDS, 4),
+        (ROUNDS,), (ROUNDS, 6), (ROUNDS, 4), (ROUNDS, 4),
         (CAP,), (CAP,), (6,), (6,), (1,), (1,), (2, 6), (2, 6), (CAP,),
     ]
     return pl.pallas_call(

time: 149 us -> 149 us (level)
  no operation moved by 1% of the time
where the time goes in v8:
time: 149 us
  Pallas kernels  148 us (99%)
    pallas_call x1, Pallas kernels, gradient_blocks(): pl.pallas_call(gradient_kernel, out_shape=(jax.ShapeDtypeStruct((CAP, BLK...  141 us
    pallas_call x1, Pallas kernels, grams(): pl.pallas_call(grams_kernel, in_specs=[pl.BlockSpec(memory_space=pl.ANY)]...  6.63 us

profile of v8, /device:TPU:1, one launch (start us, length us, event | category | flops | bytes accessed | tf_op | source)
XLA Modules:
  0.0 148.6 jit_solution(6491431251918583988)
XLA Ops:
  0.6 141.2 %gradient_blocks.1 = (bf16[3,512,512]{2,1,0:T(8,128)(2,1)}, bf16[2,512,512]{2,1,0:T(8,128)(2,1)}) custom-call(s32[16]{0:T(128)} %bitcast.1, bf16[512,512]{1,0:T(8,128)(2,1)} %acts_ref.1, bf16[512,2048]{1,0:T(8,128)(2,1)} %grads_ref.1, bf16[1,1,3,512,512]{4,3,2,1,0:T(8,128)(2,1)} %lr_ref.1, bf16[1,1,3,512,512]{4,3,2,1,0:T(8,128)(2,1)} %rr_ref.1), custom_call_target="tpu_custom_call" | custom-call | flops 12884901888 | bytes 10485760 | tf_op jit(solution)/shard_map/gradient_blocks/pallas_call | solution.py:495
  141.8 6.6 %grams.1 = (f32[1,1,3,512,512]{4,3,2,1,0:T(8,128)}, f32[1,1,3,512,512]{4,3,2,1,0:T(8,128)}, bf16[2,512,512]{2,1,0:T(8,128)(2,1)}) custom-call(bf16[3,512,512]{2,1,0:T(8,128)(2,1)} %get-tuple-element.5.owned_ref, f32[1,1,3,512,512]{4,3,2,1,0:T(8,128)} %ls_ref.1, f32[1,1,3,512,512]{4,3,2,1,0:T(8,128)} %rs_ref.1, bf16[2,512,512]{2,1,0:T(8,128)(2,1)} %get-tuple-element.6.held_ref), custom_call_target="tpu_custom_call" | custom-call | tf_op jit(solution)/shard_map/grams/pallas_call | solution.py:551
